TPU v7x, 32 devices: a whole 2x2x4 slice. The times are simulated.
32 devices in a mesh: section: 2 (over core), dp: 4 (over z), ns: 4 (over y, x).
Axes of the slice: x: 2, y: 2, z: 4, core: 2. Of those that a mesh axis runs over, the one named last changes fastest.
Arguments:
- inputs: bfloat16 [32, 1024, 512], P(('dp', 'ns')), may hold values from -6 to 6
- cotangent: bfloat16 [32, 1024, 512], P(('dp', 'ns')), may hold values from -6 to 6
- lengths: int32 [32], P(('dp', 'ns')), may hold values from 256 to 1024, as said below
- species: int32 [32], P(('dp', 'ns')), may hold values from 0 to 7
- conv_weight: float32 [2, 4608, 512], P('section', 'ns'), may hold values from -0.09375 to 0.09375
- up_weight: float32 [2, 512, 2048], P('section', None, 'ns'), may hold values from -0.25 to 0.25
- down_weight: float32 [2, 2048, 512], P('section', 'ns'), may hold values from -0.125 to 0.125
- conv_moment: float32 [2, 4608, 512], P('section', 'ns')
- up_moment: float32 [2, 512, 2048], P('section', None, 'ns')
- down_moment: float32 [2, 2048, 512], P('section', 'ns')
- vec_values: float32 [2, 10, 512], P('section')
- vec_first: float32 [2, 10, 512], P('section')
- vec_second: float32 [2, 10, 512], P('section')
- head_weight: bfloat16 [512, 6], replicated, may hold values from -0.375 to 0.375
- head_bias: float32 [6], replicated, may hold values from -4 to 4
Outputs:
- activations: bfloat16 [2, 32, 1024, 512], P('section', ('dp', 'ns'))
- input_grad: bfloat16 [2, 32, 1024, 512], P('section', ('dp', 'ns'))
- conv_grad: float32 [2, 4608, 512], P('section', 'ns')
- up_grad: float32 [2, 512, 2048], P('section', None, 'ns')
- down_grad: float32 [2, 2048, 512], P('section', 'ns')
- conv_momentum: float32 [2, 4608, 512], P('section', 'ns')
- up_momentum: float32 [2, 512, 2048], P('section', None, 'ns')
- down_momentum: float32 [2, 2048, 512], P('section', 'ns')
- conv_new: float32 [2, 4608, 512], P('section', 'ns')
- up_new: float32 [2, 512, 2048], P('section', None, 'ns')
- down_new: float32 [2, 2048, 512], P('section', 'ns')
- conv_copy: bfloat16 [2, 4608, 512], P('section', 'ns')
- up_copy: bfloat16 [2, 512, 2048], P('section', None, 'ns')
- down_copy: bfloat16 [2, 2048, 512], P('section', 'ns')
- vec_grad: float32 [2, 10, 512], P('section')
- vec_first_new: float32 [2, 10, 512], P('section')
- vec_second_new: float32 [2, 10, 512], P('section')
- vec_new: float32 [2, 10, 512], P('section')
- species_freq: float32 [2, 8, 6], P('section')
- species_share: float32 [2, 8], P('section')
Inputs may be any that keep to these rules, and one draw needn't show every extreme that they name: `lengths`: each length is 256, 512 or 1024; the first window has 256 and the last 1024.
All inputs are finite; a program needn't handle non-finite values.
Results may differ from a plain program's by a relative error of at most 0.011.
Values may be sent and summed in bfloat16 or wider, within the bound.
No kernel may reach another device: no remote copies, remote signals or barrier semaphores. Data moves between devices by JAX's collectives and lax.ppermute only.
A program may use at most 320 MiB of HBM per device.

v0:
```python
import math

import jax
import jax.numpy as jnp
from jax import lax
from jax.sharding import PartitionSpec as P

D = 512
FF = 2048
SECOND_DILATION = 32
SPECIES = 8
STEP = 10


PRECISE = lax.Precision.HIGHEST
NORM_EPSILON = 1e-05
GRAM_EPSILON = 1e-07
ADAM_EPSILON = 1e-08
SCHULZ_LINEAR = 3.4445
SCHULZ_CUBIC = -4.775
SCHULZ_QUINTIC = 2.0315
MUON_MOMENTUM = 0.5
MUON_RATE = 0.1
MUON_DECAY = 0.01
ADAM_RATE = 0.5
ADAM_DECAY = 0.01
BETA_ONE = 0.9
BETA_TWO = 0.95


def shifted(value, axis, steps):
    count = lax.axis_size(axis)
    leading, last = (max(0, -steps), min(count, count - steps))
    return lax.ppermute(value, axis, [(source, source + steps) for source in range(leading, last)])


def layer_norm(feature_maps, gain_vec, bias_vec):
    average = jnp.mean(feature_maps, axis=-1, keepdims=True)
    centred = feature_maps - average
    variance = jnp.mean(centred * centred, axis=-1, keepdims=True)
    return centred * lax.rsqrt(variance + NORM_EPSILON) * gain_vec + bias_vec


def first_piece(conv_out, values_in, gain_vec, bias_vec):
    return values_in + layer_norm(jax.nn.gelu(conv_out), gain_vec, bias_vec)


def second_piece(branch_out, middle, gain_vec, bias_vec):
    return middle + layer_norm(branch_out, gain_vec, bias_vec)


def spread_taps(masked, tap_spacing):
    win_len = masked.shape[0]
    edge_margin = 4 * SECOND_DILATION
    padded = jnp.pad(masked, ((edge_margin, edge_margin), (0, 0)))
    pieces = [
        lax.dynamic_slice_in_dim(padded, edge_margin + (tap_index - 4) * tap_spacing, win_len, 0)
        for tap_index in range(9)
    ]
    return jnp.concatenate(pieces, axis=1)


def collect_taps(spread_grad, tap_spacing):
    win_len = spread_grad.shape[0]
    feature = spread_grad.shape[1] // 9
    edge_margin = 4 * SECOND_DILATION
    summed = jnp.zeros((win_len, feature), jnp.float32)
    for tap_index in range(9):
        column_block = jnp.pad(
            spread_grad[:, tap_index * feature : (tap_index + 1) * feature],
            ((edge_margin, edge_margin), (0, 0)),
        )
        summed = summed + lax.dynamic_slice_in_dim(
            column_block, edge_margin - (tap_index - 4) * tap_spacing, win_len, 0
        )
    return summed


def contract_rows(left, right):
    return lax.dot_general(
        left, right, (((0,), (0,)), ((), ())), preferred_element_type=jnp.float32
    )


def contract_cols(left, right):
    return lax.dot_general(
        left, right, (((1,), (1,)), ((), ())), preferred_element_type=jnp.float32
    )


def tall_gram(matrix):
    return lax.dot_general(
        matrix,
        matrix,
        (((0,), (0,)), ((), ())),
        precision=PRECISE,
        preferred_element_type=jnp.float32,
    )


def wide_gram(matrix):
    return lax.dot_general(
        matrix,
        matrix,
        (((1,), (1,)), ((), ())),
        precision=PRECISE,
        preferred_element_type=jnp.float32,
    )


def schulz_poly(gram_mat):
    return SCHULZ_CUBIC * gram_mat + SCHULZ_QUINTIC * jnp.dot(
        gram_mat, gram_mat, precision=PRECISE, preferred_element_type=jnp.float32
    )


def tall_turn(matrix, gram_mat):
    return SCHULZ_LINEAR * matrix + jnp.dot(
        matrix, schulz_poly(gram_mat), precision=PRECISE, preferred_element_type=jnp.float32
    )


def wide_turn(matrix, gram_mat):
    return SCHULZ_LINEAR * matrix + jnp.dot(
        schulz_poly(gram_mat), matrix, precision=PRECISE, preferred_element_type=jnp.float32
    )


def forward(block_input, padding_mask, tap_spacing, matrices, vectors):
    conv_full, up_full, down_full = matrices
    masked = block_input * padding_mask[:, None].astype(jnp.bfloat16)
    stacked = spread_taps(masked, tap_spacing)
    conv_out = jnp.dot(stacked, conv_full, preferred_element_type=jnp.float32) + vectors[0]
    middle = first_piece(conv_out, block_input.astype(jnp.float32), vectors[1], vectors[2])
    middle_low = middle.astype(jnp.bfloat16)
    hidden_pre = jnp.dot(middle_low, up_full, preferred_element_type=jnp.float32) + vectors[
        3:7
    ].reshape(-1)
    hidden = jax.nn.gelu(hidden_pre).astype(jnp.bfloat16)
    branch_out = jnp.dot(hidden, down_full, preferred_element_type=jnp.float32) + vectors[7]
    block_out = second_piece(branch_out, middle, vectors[8], vectors[9]).astype(jnp.bfloat16)
    return (block_out, (stacked, conv_out, middle, middle_low, hidden_pre, hidden, branch_out))


def backward(context, grad_out, block_input, padding_mask, tap_spacing, matrices, vectors):
    conv_full, up_full, down_full = matrices
    stacked, conv_out, middle, middle_low, hidden_pre, hidden, branch_out = context
    feature = vectors.shape[1]
    unused, pull_two = jax.vjp(second_piece, branch_out, middle, vectors[8], vectors[9])
    d_out, d_middle_res, d_gain_two, d_shift_two = pull_two(grad_out)
    d_out_low = d_out.astype(jnp.bfloat16)
    g_down = contract_rows(hidden, d_out_low)
    d_hidden = contract_cols(d_out_low, down_full)
    unused_pre, pull_gelu = jax.vjp(jax.nn.gelu, hidden_pre)
    (d_pre,) = pull_gelu(d_hidden)
    d_pre_low = d_pre.astype(jnp.bfloat16)
    g_up = contract_rows(middle_low, d_pre_low)
    d_middle = d_middle_res + contract_cols(d_pre_low, up_full)
    unused_conv, pull_one = jax.vjp(
        first_piece, conv_out, block_input.astype(jnp.float32), vectors[1], vectors[2]
    )
    d_conv, d_input_res, d_gain_one, d_shift_one = pull_one(d_middle)
    d_conv_low = d_conv.astype(jnp.bfloat16)
    g_conv = contract_rows(stacked, d_conv_low)
    d_stacked = contract_cols(d_conv_low, conv_full)
    d_input = d_input_res + collect_taps(d_stacked, tap_spacing) * padding_mask[:, None]
    g_vec = jnp.concatenate(
        [
            jnp.sum(d_conv_low, axis=0, dtype=jnp.float32)[None],
            d_gain_one[None],
            d_shift_one[None],
            jnp.sum(d_pre_low, axis=0, dtype=jnp.float32).reshape(4, feature),
            jnp.sum(d_out_low, axis=0, dtype=jnp.float32)[None],
            d_gain_two[None],
            d_shift_two[None],
        ],
        axis=0,
    )
    return (d_input.astype(jnp.bfloat16), (g_conv, g_up, g_down, g_vec))


def on_device(
    inputs,
    cotangent,
    lengths,
    species,
    conv_weight,
    up_weight,
    down_weight,
    conv_moment,
    up_moment,
    down_moment,
    vec_values,
    vec_first,
    vec_second,
    head_weight,
    head_bias,
):
    opening_section = lax.axis_index("section") == 0
    tap_spacing = jnp.where(opening_section, 1, SECOND_DILATION).astype(jnp.int32)
    matrices = (
        lax.all_gather(conv_weight[0].astype(jnp.bfloat16), "ns", axis=0, tiled=True),
        lax.all_gather(up_weight[0].astype(jnp.bfloat16), "ns", axis=1, tiled=True),
        lax.all_gather(down_weight[0].astype(jnp.bfloat16), "ns", axis=0, tiled=True),
    )
    vectors = vec_values[0]
    batches = inputs.shape[0]
    win_len = inputs.shape[1]
    positions = jnp.arange(win_len)
    species_range = jnp.arange(SPECIES)
    prob_sums = jnp.zeros((SPECIES, head_weight.shape[1]), jnp.float32)
    token_counts = jnp.zeros((SPECIES,), jnp.float32)
    received = jnp.zeros_like(inputs[0])
    tick_inputs = []
    tick_outputs = []
    tick_states = []
    for tick_index in range(batches + 1):
        own_batch = min(tick_index, batches - 1)
        earlier = max(tick_index - 1, 0)
        block_input = jnp.where(opening_section, inputs[own_batch], received)
        length = jnp.where(opening_section, lengths[own_batch], lengths[earlier])
        species_id = jnp.where(opening_section, species[own_batch], species[earlier])
        counted = jnp.where(opening_section, tick_index < batches, tick_index >= 1).astype(
            jnp.float32
        )
        padding_mask = (positions < length).astype(jnp.float32)
        block_out, context = forward(block_input, padding_mask, tap_spacing, matrices, vectors)
        logits = jnp.dot(block_out, head_weight, preferred_element_type=jnp.float32) + head_bias
        chances = jax.nn.softmax(logits, axis=-1)
        weighted = jnp.sum(chances * padding_mask[:, None], axis=0)
        species_hit = (species_range == species_id).astype(jnp.float32) * counted
        prob_sums = prob_sums + species_hit[:, None] * weighted[None, :]
        token_counts = token_counts + species_hit * jnp.sum(padding_mask)
        tick_inputs.append(block_input)
        tick_outputs.append(block_out)
        tick_states.append(context)
        if tick_index < batches:
            received = shifted(block_out, "section", 1)
    input_stack = jnp.stack(tick_inputs)
    activations = jnp.stack(
        [
            jnp.where(opening_section, tick_outputs[batch_index], tick_outputs[batch_index + 1])
            for batch_index in range(batches)
        ]
    )
    feature = vectors.shape[1]
    gradients = (
        jnp.zeros((9 * feature, feature), jnp.float32),
        jnp.zeros((feature, 4 * feature), jnp.float32),
        jnp.zeros((4 * feature, feature), jnp.float32),
        jnp.zeros((10, feature), jnp.float32),
    )
    back_received = jnp.zeros_like(inputs[0])
    tick_grads = []
    for tick_index in range(batches + 1):
        late_batch = min(tick_index, batches - 1)
        early_batch = max(tick_index - 1, 0)
        source_tick = jnp.where(opening_section, early_batch, late_batch + 1)
        length = jnp.where(opening_section, lengths[early_batch], lengths[late_batch])
        padding_mask = (positions < length).astype(jnp.float32)
        counted = jnp.where(opening_section, tick_index >= 1, tick_index < batches).astype(
            jnp.float32
        )
        grad_out = jnp.where(
            opening_section,
            back_received.astype(jnp.float32),
            cotangent[late_batch].astype(jnp.float32) * padding_mask[:, None],
        )
        block_input = lax.dynamic_index_in_dim(input_stack, source_tick, 0, keepdims=False)
        context = forward(block_input, padding_mask, tap_spacing, matrices, vectors)[1]
        tick_input_grad, tick_terms = backward(
            context, grad_out, block_input, padding_mask, tap_spacing, matrices, vectors
        )
        gradients = tuple(
            (running + counted * tick_term for running, tick_term in zip(gradients, tick_terms))
        )
        tick_grads.append(tick_input_grad)
        if tick_index < batches:
            back_received = shifted(tick_input_grad, "section", -1)
    input_grad = jnp.stack(
        [
            jnp.where(opening_section, tick_grads[batch_index + 1], tick_grads[batch_index])
            for batch_index in range(batches)
        ]
    )
    conv_rows, up_cols, down_rows = (
        lax.psum_scatter(gradients[0], "ns", scatter_dimension=0, tiled=True),
        lax.psum_scatter(gradients[1], "ns", scatter_dimension=1, tiled=True),
        lax.psum_scatter(gradients[2], "ns", scatter_dimension=0, tiled=True),
    )
    conv_grad, up_grad, down_grad, vec_part = lax.psum(
        (conv_rows, up_cols, down_rows, gradients[3]), "dp"
    )
    conv_state = MUON_MOMENTUM * conv_moment[0] + conv_grad
    up_state = MUON_MOMENTUM * up_moment[0] + up_grad
    down_state = MUON_MOMENTUM * down_moment[0] + down_grad
    conv_square, up_square, down_square, vec_grad = lax.psum(
        (
            jnp.sum(conv_state * conv_state),
            jnp.sum(up_state * up_state),
            jnp.sum(down_state * down_state),
            vec_part,
        ),
        "ns",
    )
    conv_orth = conv_state * lax.rsqrt(conv_square + GRAM_EPSILON)
    up_orth = up_state * lax.rsqrt(up_square + GRAM_EPSILON)
    down_orth = down_state * lax.rsqrt(down_square + GRAM_EPSILON)
    for sweep_index in range(5):
        conv_gram, up_gram, down_gram = lax.psum(
            (tall_gram(conv_orth), wide_gram(up_orth), tall_gram(down_orth)), "ns"
        )
        conv_orth = tall_turn(conv_orth, conv_gram)
        up_orth = wide_turn(up_orth, up_gram)
        down_orth = tall_turn(down_orth, down_gram)
    keep_factor = 1.0 - MUON_RATE * MUON_DECAY
    conv_next = conv_weight[0] * keep_factor - MUON_RATE * 0.2 * math.sqrt(9 * D) * conv_orth
    up_next = up_weight[0] * keep_factor - MUON_RATE * 0.2 * math.sqrt(FF) * up_orth
    down_next = down_weight[0] * keep_factor - MUON_RATE * 0.2 * math.sqrt(FF) * down_orth
    first_next = BETA_ONE * vec_first[0] + (1.0 - BETA_ONE) * vec_grad
    second_next = BETA_TWO * vec_second[0] + (1.0 - BETA_TWO) * vec_grad * vec_grad
    vec_next = vectors * (1.0 - ADAM_RATE * ADAM_DECAY) - ADAM_RATE * (
        first_next / (1.0 - BETA_ONE**STEP)
    ) / (jnp.sqrt(second_next / (1.0 - BETA_TWO**STEP)) + ADAM_EPSILON)
    prob_total, count_total = lax.psum((prob_sums, token_counts), ("dp", "ns"))
    species_freq = prob_total / jnp.maximum(count_total, 1.0)[:, None]
    species_share = SPECIES * count_total / jnp.sum(count_total)
    return (
        activations[None],
        input_grad[None],
        conv_grad[None],
        up_grad[None],
        down_grad[None],
        conv_state[None],
        up_state[None],
        down_state[None],
        conv_next[None],
        up_next[None],
        down_next[None],
        conv_next.astype(jnp.bfloat16)[None],
        up_next.astype(jnp.bfloat16)[None],
        down_next.astype(jnp.bfloat16)[None],
        vec_grad[None],
        first_next[None],
        second_next[None],
        vec_next[None],
        species_freq[None],
        species_share[None],
    )


def solution(mesh):
    placed = (
        P(("dp", "ns"), None, None),
        P(("dp", "ns"), None, None),
        P(("dp", "ns")),
        P(("dp", "ns")),
        P("section", "ns", None),
        P("section", None, "ns"),
        P("section", "ns", None),
        P("section", "ns", None),
        P("section", None, "ns"),
        P("section", "ns", None),
        P("section", None, None),
        P("section", None, None),
        P("section", None, None),
        P(),
        P(),
    )
    return jax.shard_map(
        on_device,
        mesh=mesh,
        in_specs=placed,
        out_specs=(
            P("section", ("dp", "ns"), None, None),
            P("section", ("dp", "ns"), None, None),
            P("section", "ns", None),
            P("section", None, "ns"),
            P("section", "ns", None),
            P("section", "ns", None),
            P("section", None, "ns"),
            P("section", "ns", None),
            P("section", "ns", None),
            P("section", None, "ns"),
            P("section", "ns", None),
            P("section", "ns", None),
            P("section", None, "ns"),
            P("section", "ns", None),
            P("section", None, None),
            P("section", None, None),
            P("section", None, None),
            P("section", None, None),
            P("section", None, None),
            P("section", None),
        ),
        check_vma=False,
    )
```

profile of v0, /device:TPU:0, one launch (start us, length us, event | category | flops | bytes accessed | tf_op | source)
XLA Modules:
  0.0 1477.3 jit_solution(6849727618815460939)
XLA Ops:
  26.6 43.6 %all-gather.7.cloned.1.call-done = bf16[1,4608,512]{2,1,0:T(8,128)(2,1)} async-done(((bf16[1,1152,512]{2,1,0:T(8,128)(2,1)}), bf16[1,4608,512]{2,1,0:T(8,128)(2,1)}) %all-gather.7.cloned.1.call-update) | async-done | bytes 4718608 | tf_op jit(solution)/shard_map/all_gather | solution.py:202
  70.3 10.1 fusion.372
  80.7 27.2 %all-gather.9.cloned.1.call-done = bf16[1,512,2048]{2,1,0:T(8,128)(2,1)} async-done(((bf16[1,512,512]{2,1,0:T(8,128)(2,1)}), bf16[1,512,2048]{2,1,0:T(8,128)(2,1)}) %all-gather.9.cloned.1.call-update) | async-done | bytes 2097168 | tf_op jit(solution)/shard_map/all_gather | solution.py:203
  107.9 37.8 %all-gather.11.cloned.1.call-done = bf16[1,2048,512]{2,1,0:T(8,128)(2,1)} async-done(((bf16[1,512,512]{2,1,0:T(8,128)(2,1)}), bf16[1,2048,512]{2,1,0:T(8,128)(2,1)}) %all-gather.11.cloned.1.call-update) | async-done | bytes 2097168 | tf_op jit(solution)/shard_map/all_gather | solution.py:204
  145.6 9.5 add_reduce_fusion.5
  172.7 5.6 fusion.377
  179.9 10.9 add_reduce_fusion.4
  227.4 8.4 fusion.382
  263.4 7.2 fusion.55
  270.7 9.9 fusion.51
  280.6 9.8 fusion.352
  296.9 10.5 multiply_convert_fusion.1
  307.4 4.6 add_reduce_fusion.2
  324.8 13.7 fusion.159
  338.5 3.9 fusion.363
  344.0 10.9 convert_reduce_fusion.2
  354.9 4.0 fusion.353
  365.4 9.2 fusion.45
  374.6 9.3 fusion.366
  383.9 7.1 fusion.84
  392.5 5.3 fusion.349
  403.1 10.4 convert_reduce_fusion.1
  422.6 9.6 fusion.49
  432.2 9.3 fusion.365
  441.5 8.0 select_bitcast_fusion.1
  450.8 7.5 fusion.351
  462.8 8.3 convert_reduce_fusion
  473.1 7.0 multiply_add_fusion.2
  480.3 5.1 fusion.392
  488.0 6.2 multiply_add_fusion.1
  494.2 10.5 fusion.390
  504.8 11.5 fusion.391
  525.4 12.6 multiply_add_fusion
  538.1 51.7 %reduce-scatter.8.cloned.1.call-done = f32[512,512]{1,0:T(8,128)} async-done(((f32[2048,512]{1,0:T(8,128)}), f32[512,512]{1,0:T(8,128)}) %reduce-scatter.8.cloned.1.call-update) | async-done | bytes 1048592 | tf_op jit(solution)/shard_map/reduce_scatter | solution.py:289
  589.8 98.0 %reduce-scatter.4.cloned.1.call-done = f32[1152,512]{1,0:T(8,128)} async-done(((f32[4608,512]{1,0:T(8,128)}), f32[1152,512]{1,0:T(8,128)}) %reduce-scatter.4.cloned.1.call-update) | async-done | bytes 2359312 | tf_op jit(solution)/shard_map/reduce_scatter | solution.py:287
  688.8 19.8 %psum.196 = f32[10,512]{1,0:T(8,128)S(1)} all-reduce(f32[10,512]{1,0:T(8,128)S(1)} %multiply_add_fusion.3), channel_id=1, replica_groups=mesh['section'=2,'dp'=4,'ns'=4] {'dp'}, use_global_device_ids=true, to_apply=%region_84.85 | all-reduce | flops 5120 | bytes 40960 | tf_op jit(solution)/shard_map/psum | solution.py:291
  708.6 146.4 %all-reduce.55.cloned.1.call-done = (f32[1152,512]{1,0:T(8,128)}, f32[512,512]{1,0:T(8,128)}, f32[512,512]{1,0:T(8,128)}) async-done(((f32[1152,512]{1,0:T(8,128)}, f32[512,512]{1,0:T(8,128)}, f32[512,512]{1,0:T(8,128)}), (f32[1152,512]{1,0:T(8,128)}, f32[512,512]{1,0:T(8,128)}, f32[512,512]{1,0:T(8,128)})) %all-reduce.55.cloned.1.call-update) | async-done | bytes 4456464 | tf_op jit(solution)/shard_map/psum | solution.py:291
  861.0 17.7 %all-reduce.31 = (f32[]{:T(128)}, f32[]{:T(128)}, f32[]{:T(128)}, f32[10,512]{1,0:T(8,128)S(1)}) all-reduce(f32[]{:T(128)} %get-tuple-element.118, f32[]{:T(128)} %get-tuple-element.116, f32[]{:T(128)} %get-tuple-element.114, f32[10,512]{1,0:T(8,128)S(1)} %psum.196), channel_id=1, replica_groups=mesh['section'=2,'dp'=4,'ns'=4] {'ns'}, use_global_device_ids=true, to_apply=%region_43.44 | all-reduce | flops 5123 | bytes 40984 | tf_op jit(solution)/shard_map/psum | solution.py:297
  880.8 5.3 fusion.71
  892.1 84.7 %all-reduce.53.cloned.1.call-done = (f32[512,512]{1,0:T(8,128)}, f32[512,512]{1,0:T(8,128)}, f32[512,512]{1,0:T(8,128)}) async-done(((f32[512,512]{1,0:T(8,128)}, f32[512,512]{1,0:T(8,128)}, f32[512,512]{1,0:T(8,128)}), (f32[512,512]{1,0:T(8,128)}, f32[512,512]{1,0:T(8,128)}, f32[512,512]{1,0:T(8,128)})) %all-reduce.53.cloned.1.call-update) | async-done | bytes 3145744 | tf_op jit(solution)/shard_map/psum | solution.py:310
  976.8 3.8 fusion.241
  995.3 4.0 convolution_add_fusion.4
  999.3 5.4 fusion.394
  1005.1 87.3 %all-reduce.51.cloned.1.call-done = (f32[512,512]{1,0:T(8,128)}, f32[512,512]{1,0:T(8,128)}, f32[512,512]{1,0:T(8,128)}) async-done(((f32[512,512]{1,0:T(8,128)}, f32[512,512]{1,0:T(8,128)}, f32[512,512]{1,0:T(8,128)}), (f32[512,512]{1,0:T(8,128)}, f32[512,512]{1,0:T(8,128)}, f32[512,512]{1,0:T(8,128)})) %all-reduce.51.cloned.1.call-update) | async-done | bytes 3145744 | tf_op jit(solution)/shard_map/psum | solution.py:310
  1092.4 3.8 fusion.240
  1096.2 4.0 convolution_add_fusion.3
  1100.3 5.3 fusion.395
  1128.6 79.3 %all-reduce.49.cloned.1.call-done = (f32[512,512]{1,0:T(8,128)}, f32[512,512]{1,0:T(8,128)}, f32[512,512]{1,0:T(8,128)}) async-done(((f32[512,512]{1,0:T(8,128)}, f32[512,512]{1,0:T(8,128)}, f32[512,512]{1,0:T(8,128)}), (f32[512,512]{1,0:T(8,128)}, f32[512,512]{1,0:T(8,128)}, f32[512,512]{1,0:T(8,128)})) %all-reduce.49.cloned.1.call-update) | async-done | bytes 3145744 | tf_op jit(solution)/shard_map/psum | solution.py:310
  1207.9 3.9 fusion.239
  1211.8 6.4 convolution_add_fusion.2
  1218.3 5.4 fusion.396
  1242.4 5.0 select_bitcast_fusion.2
  1249.0 3.9 copy.72
  1254.6 40.9 %all-reduce.30 = (f32[8,6]{1,0:T(8,128)S(1)}, f32[8]{0:T(128)S(1)}) all-reduce(f32[8,6]{1,0:T(8,128)S(1)} %multiply_add_fusion.4, f32[8]{0:T(128)S(1)} %get-tuple-element.96), channel_id=1, replica_groups=mesh['section'=2,'dp'=4,'ns'=4] {'dp','ns'}, use_global_device_ids=true, to_apply=%region_95.96 | all-reduce | flops 56 | bytes 448 | tf_op jit(solution)/shard_map/psum | solution.py:325
  1298.0 29.4 %all-reduce.47.cloned.1.call-done = (f32[512,512]{1,0:T(8,128)}, f32[512,512]{1,0:T(8,128)}, f32[512,512]{1,0:T(8,128)}) async-done(((f32[512,512]{1,0:T(8,128)}, f32[512,512]{1,0:T(8,128)}, f32[512,512]{1,0:T(8,128)}), (f32[512,512]{1,0:T(8,128)}, f32[512,512]{1,0:T(8,128)}, f32[512,512]{1,0:T(8,128)})) %all-reduce.47.cloned.1.call-update) | async-done | bytes 3145744 | tf_op jit(solution)/shard_map/psum | solution.py:310
  1327.5 3.9 fusion.238
  1331.4 4.0 convolution_add_fusion.1
  1335.4 5.3 fusion.397
  1356.7 7.2 fusion.53
  1363.9 6.0 fusion.364
  1369.9 8.4 select_bitcast_fusion
  1383.9 59.3 %all-reduce.45.cloned.1.call-done = (f32[512,512]{1,0:T(8,128)}, f32[512,512]{1,0:T(8,128)}, f32[512,512]{1,0:T(8,128)}) async-done(((f32[512,512]{1,0:T(8,128)}, f32[512,512]{1,0:T(8,128)}, f32[512,512]{1,0:T(8,128)}), (f32[512,512]{1,0:T(8,128)}, f32[512,512]{1,0:T(8,128)}, f32[512,512]{1,0:T(8,128)})) %all-reduce.45.cloned.1.call-update) | async-done | bytes 3145744 | tf_op jit(solution)/shard_map/psum | solution.py:310
  1443.2 4.0 fusion.237
  1447.3 6.2 fusion.70
  (577 shorter events, 274.1 us)
Async XLA Ops:
  7.2 1231.4 %copy-start = (bf16[512,6]{0,1:T(8,128)(2,1)S(1)}, bf16[512,6]{0,1:T(8,128)(2,1)}, u32[]{:S(2)}) copy-start(bf16[512,6]{0,1:T(8,128)(2,1)} %param.28) | copy-start | bytes 18436
  7.2 63.1 %all-gather.7.cloned.1.call-start = ((), (), s32[]{:S(2)}) async-start(), calls=%async_computation.6 | async-start | bytes 5898240 | tf_op jit(solution)/shard_map/all_gather | solution.py:202
  10.2 97.6 %all-gather.9.cloned.1.call-start = ((), (), s32[]{:S(2)}) async-start(), calls=%async_computation.7 | async-start | bytes 2621440 | tf_op jit(solution)/shard_map/all_gather | solution.py:203
  11.2 134.5 %all-gather.11.cloned.1.call-start = ((), (), s32[]{:S(2)}) async-start(), calls=%async_computation.8 | async-start | bytes 2621440 | tf_op jit(solution)/shard_map/all_gather | solution.py:204
  12.5 525.6 %reduce-scatter.6.cloned.1.call-start = ((), (), s32[]{:S(2)}) async-start(), calls=%async_computation.4 | async-start | bytes 5242880 | tf_op jit(solution)/shard_map/reduce_scatter | solution.py:288
  26.6 166.2 %copy-start.104 = (f32[1,1,512]{2,0,1:T(1,128)}, f32[1,1,512]{2,0,1:T(1,128)S(1)}, u32[]{:S(2)}) copy-start(f32[1,1,512]{2,0,1:T(1,128)S(1)} %get-tuple-element.174) | copy-start | bytes 6148
  80.3 74.8 %copy-start.40 = (f32[1024,512]{0,1:T(8,128)}, f32[1024,512]{0,1:T(8,128)S(1)}, u32[]{:S(2)}) copy-start(f32[1024,512]{0,1:T(8,128)S(1)} %get-tuple-element.185) | copy-start | bytes 6291460
  159.8 33.1 %copy-start.35 = (bf16[1024,512]{0,1:T(8,128)(2,1)}, bf16[1024,512]{0,1:T(8,128)(2,1)S(1)}, u32[]{:S(2)}) copy-start(bf16[1024,512]{0,1:T(8,128)(2,1)S(1)} %add_convert_fusion.8) | copy-start | bytes 3145732
  159.8 5.7 collective-permute-start
  196.7 13.6 collective-permute-start.1
  208.4 175.5 %copy-start.92 = (f32[1024]{0:T(1024)}, f32[1024]{0:T(1024)S(1)}, u32[]{:S(2)}) copy-start(f32[1024]{0:T(1024)S(1)} %fusion.316) | copy-start | bytes 12292
  210.5 114.3 %copy-start.36 = (bf16[1024,512]{0,1:T(8,128)(2,1)}, bf16[1024,512]{0,1:T(8,128)(2,1)S(1)}, u32[]{:S(2)}) copy-start(bf16[1024,512]{0,1:T(8,128)(2,1)S(1)} %get-tuple-element.133) | copy-start | bytes 3145732
  211.8 100.6 %copy-start.24 = (bf16[3,1024,512]{1,2,0:T(8,128)(2,1)}, bf16[3,1024,512]{1,2,0:T(8,128)(2,1)S(1)}, u32[]{:S(2)}) copy-start(bf16[3,1024,512]{1,2,0:T(8,128)(2,1)S(1)} %pad_maximum_fusion) | copy-start | bytes 9437188
  215.8 11.6 slice-start.8
  235.8 89.1 %copy-start.96 = (f32[1024]{0:T(1024)}, f32[1024]{0:T(1024)S(1)}, u32[]{:S(2)}) copy-start(f32[1024]{0:T(1024)S(1)} %broadcast_multiply_fusion.9) | copy-start | bytes 12292
  236.1 88.8 %copy-start.108 = (f32[1024]{0:T(1024)}, f32[1024]{0:T(1024)S(1)}, u32[]{:S(2)}) copy-start(f32[1024]{0:T(1024)S(1)} %add_rsqrt_fusion.1) | copy-start | bytes 12292
  241.6 21.8 %copy-start.85 = (bf16[1024,4608]{0,1:T(8,128)(2,1)}, bf16[1024,4608]{0,1:T(8,128)(2,1)S(1)}, u32[]{:S(2)}) copy-start(bf16[1024,4608]{0,1:T(8,128)(2,1)S(1)} %fusion.279) | copy-start | bytes 28311556
  263.4 17.1 %slice-start = ((s8[9437184]{0:T(1024)(128)(4,1)}), s8[1048576]{0:T(1024)(128)(4,1)S(1)}, s32[]{:S(2)}) async-start(s8[9437184]{0:T(1024)(128)(4,1)} %bitcast.457), calls=%async_computation.15 | async-start | bytes 2097152
  263.4 17.1 %slice-start.1 = ((s8[9437184]{0:T(1024)(128)(4,1)}), s8[4194304]{0:T(1024)(128)(4,1)S(1)}, s32[]{:S(2)}) async-start(s8[9437184]{0:T(1024)(128)(4,1)} %bitcast.457), calls=%async_computation.16 | async-start | bytes 8388608
  270.7 22.8 %copy-start.11 = (f32[1024,512]{0,1:T(8,128)}, f32[1024,512]{0,1:T(8,128)S(1)}, u32[]{:S(2)}) copy-start(f32[1024,512]{0,1:T(8,128)S(1)} %fusion.55) | copy-start | bytes 6291460
  280.6 16.2 %copy-start.9 = (f32[1024,512]{0,1:T(8,128)}, f32[1024,512]{0,1:T(8,128)S(1)}, u32[]{:S(2)}) copy-start(f32[1024,512]{0,1:T(8,128)S(1)} %fusion.51) | copy-start | bytes 6291460
  290.4 22.1 %copy-start.7 = (f32[1024,512]{0,1:T(8,128)}, f32[1024,512]{0,1:T(8,128)S(1)}, u32[]{:S(2)}) copy-start(f32[1024,512]{0,1:T(8,128)S(1)} %get-tuple-element.192) | copy-start | bytes 6291460
  290.4 22.1 %copy-start.94 = (f32[1024]{0:T(1024)}, f32[1024]{0:T(1024)S(1)}, u32[]{:S(2)}) copy-start(f32[1024]{0:T(1024)S(1)} %broadcast_multiply_fusion.3) | copy-start | bytes 12292
  293.4 19.1 %copy-start.98 = (f32[1024]{0:T(1024)}, f32[1024]{0:T(1024)S(1)}, u32[]{:S(2)}) copy-start(f32[1024]{0:T(1024)S(1)} %fusion.330) | copy-start | bytes 12292
  296.9 10.6 copy-start.133
  296.9 10.6 copy-start.128
  338.5 26.9 %slice-start.10 = ((s8[4718592]{0:T(1024)(128)(4,1)}), s8[4194304]{0:T(1024)(128)(4,1)S(1)}, s32[]{:S(2)}) async-start(s8[4718592]{0:T(1024)(128)(4,1)} %bitcast.507), calls=%async_computation.25 | async-start | bytes 8388608
  343.2 11.7 copy-start.75
  344.0 10.9 copy-start.12
  344.0 10.9 copy-start.70
  344.0 10.9 copy-start.125
  344.0 21.4 %slice-start.11 = ((s8[4718592]{0:T(1024)(128)(4,1)}), s8[524288]{0:T(1024)(128)(4,1)S(1)}, s32[]{:S(2)}) async-start(s8[4718592]{0:T(1024)(128)(4,1)} %bitcast.507), calls=%async_computation.26 | async-start | bytes 1048576
  391.0 6.9 collective-permute-start.2
  399.9 22.7 %slice-start.12 = ((s8[4718592]{0:T(1024)(128)(4,1)}), s8[4194304]{0:T(1024)(128)(4,1)S(1)}, s32[]{:S(2)}) async-start(s8[4718592]{0:T(1024)(128)(4,1)} %bitcast.509), calls=%async_computation.27 | async-start | bytes 8388608
  401.7 11.8 copy-start.76
  403.1 10.4 copy-start.10
  403.1 10.4 copy-start.126
  403.1 19.5 %slice-start.13 = ((s8[4718592]{0:T(1024)(128)(4,1)}), s8[524288]{0:T(1024)(128)(4,1)S(1)}, s32[]{:S(2)}) async-start(s8[4718592]{0:T(1024)(128)(4,1)} %bitcast.509), calls=%async_computation.28 | async-start | bytes 1048576
  441.5 19.6 %slice-start.14 = ((s8[8388608]{0:T(1024)(128)(4,1)}), s8[4194304]{0:T(1024)(128)(4,1)S(1)}, s32[]{:S(2)}) async-start(s8[8388608]{0:T(1024)(128)(4,1)} %bitcast.511), calls=%async_computation.29 | async-start | bytes 8388608
  449.5 8.9 collective-permute-start.3
  450.8 10.3 slice-start.15
  462.8 10.3 copy-start.8
  462.8 10.3 copy-start.95
  462.8 10.3 copy-start.99
  462.8 10.3 copy-start.134
  480.2 109.7 %reduce-scatter.8.cloned.1.call-start = ((), (), s32[]{:S(2)}) async-start(), calls=%async_computation.5 | async-start | bytes 5242880 | tf_op jit(solution)/shard_map/reduce_scatter | solution.py:289
  494.2 193.7 %reduce-scatter.4.cloned.1.call-start = ((), (), s32[]{:S(2)}) async-start(), calls=%async_computation.3 | async-start | bytes 11796480 | tf_op jit(solution)/shard_map/reduce_scatter | solution.py:287
  494.2 10.5 copy-start.84
  504.8 11.6 copy-start.49
  504.8 11.6 copy-start.127
  504.8 11.6 copy-start.136
  504.8 20.6 %slice-start.3 = ((s8[9437184]{0:T(1024)(128)(4,1)}), s8[4194304]{0:T(1024)(128)(4,1)S(1)}, s32[]{:S(2)}) async-start(s8[9437184]{0:T(1024)(128)(4,1)} %bitcast.459), calls=%async_computation.18 | async-start | bytes 8388608
  504.8 20.6 %slice-start.4 = ((s8[9437184]{0:T(1024)(128)(4,1)}), s8[4194304]{0:T(1024)(128)(4,1)S(1)}, s32[]{:S(2)}) async-start(s8[9437184]{0:T(1024)(128)(4,1)} %bitcast.459), calls=%async_computation.19 | async-start | bytes 8388608
  538.0 317.0 %all-reduce.55.cloned.1.call-start = ((), (), s32[]{:S(2)}) async-start(), calls=%async_computation.14 | async-start | bytes 8912896 | tf_op jit(solution)/shard_map/psum | solution.py:291
  688.0 167.1 %copy-start.73 = (f32[1,512,512]{2,1,0:T(8,128)S(1)}, f32[1,512,512]{2,1,0:T(8,128)}, u32[]{:S(2)}) copy-start(f32[1,512,512]{2,1,0:T(8,128)} %param.23) | copy-start | bytes 3145732
  688.0 169.4 %copy-start.74 = (f32[1,512,512]{2,1,0:T(8,128)S(1)}, f32[1,512,512]{2,1,0:T(8,128)}, u32[]{:S(2)}) copy-start(f32[1,512,512]{2,1,0:T(8,128)} %param.24) | copy-start | bytes 3145732
  688.0 288.8 %all-reduce.53.cloned.1.call-start = ((), (), s32[]{:S(2)}) async-start(), calls=%async_computation.13 | async-start | bytes 6291456 | tf_op jit(solution)/shard_map/psum | solution.py:310
  857.3 28.8 %copy-start.30 = (f32[512,512]{1,0:T(8,128)}, f32[512,512]{1,0:T(8,128)S(1)}, u32[]{:S(2)}) copy-start(f32[512,512]{1,0:T(8,128)S(1)} %get-tuple-element.117) | copy-start | bytes 3145732
  861.0 28.0 %copy-start.28 = (f32[1152,512]{1,0:T(8,128)}, f32[1152,512]{1,0:T(8,128)S(1)}, u32[]{:S(2)}) copy-start(f32[1152,512]{1,0:T(8,128)S(1)} %get-tuple-element.119) | copy-start | bytes 7077892
  891.9 200.5 %all-reduce.51.cloned.1.call-start = ((), (), s32[]{:S(2)}) async-start(), calls=%async_computation.12 | async-start | bytes 6291456 | tf_op jit(solution)/shard_map/psum | solution.py:310
  1004.7 203.2 %all-reduce.49.cloned.1.call-start = ((), (), s32[]{:S(2)}) async-start(), calls=%async_computation.11 | async-start | bytes 6291456 | tf_op jit(solution)/shard_map/psum | solution.py:310
  1120.2 207.3 %all-reduce.47.cloned.1.call-start = ((), (), s32[]{:S(2)}) async-start(), calls=%async_computation.10 | async-start | bytes 6291456 | tf_op jit(solution)/shard_map/psum | solution.py:310
  1238.5 204.8 %all-reduce.45.cloned.1.call-start = ((), (), s32[]{:S(2)}) async-start(), calls=%async_computation.9 | async-start | bytes 6291456 | tf_op jit(solution)/shard_map/psum | solution.py:310
  1381.3 65.9 %copy-start.2 = (f32[1152,512]{1,0:T(8,128)S(1)}, f32[1152,512]{1,0:T(8,128)}, u32[]{:S(2)}) copy-start(f32[1152,512]{1,0:T(8,128)} %copy-done.1) | copy-start | bytes 7077892
  (112 other events, 392.4 us)
Sparse Core Ops, SparseCore 0:
  10.5 59.7 all-gather.6
  72.7 35.1 all-gather.8
  110.3 35.3 all-gather.10
  480.3 53.7 reduce-scatter.5
  537.1 52.6 reduce-scatter.7
  592.8 95.0 reduce-scatter.3
  690.4 164.5 all-reduce.54
  892.0 84.7 all-reduce.52
  1004.8 87.5 all-reduce.50
  1120.3 87.6 all-reduce.48
  1238.6 88.8 all-reduce.46
  1355.6 87.6 all-reduce.44
where the time goes:
time: 1490 us; the launch traced here: 1480 us
  waiting for transfers between devices  745 us (50%)
  matrix products  392 us (26%)
  local copies, waits for them, and re-layouts  131 us (9%)
  other arithmetic  98.2 us (7%)
  blocking collectives  78.4 us (5%)
  between operations  22.9 us (2%)
    psum x5, waiting for transfers between devices, on_device(): lax.psum((tall_gram(conv_orth), wide_gram(up_orth), tall_gram(down_orth))...  340 us
    psum x1, waiting for transfers between devices, on_device(): lax.psum((conv_rows, up_cols, down_rows, gradients[3]), 'dp')  146 us
    reduce_scatter x1, waiting for transfers between devices, on_device(): lax.psum_scatter(gradients[0], 'ns', scatter_dimension=0, tiled=True)  98 us
    unnamed x376, local copies, waits for them, and re-layouts  90.6 us
    dot_general x9, matrix products, contract_rows(): lax.dot_general(left, right, (((0,), (0,)), ((), ())), preferred_element_...  68.3 us
    dot_general x9, matrix products, contract_cols(): lax.dot_general(left, right, (((1,), (1,)), ((), ())), preferred_element_...  66.6 us
    reduce_scatter x1, waiting for transfers between devices, on_device(): lax.psum_scatter(gradients[2], 'ns', scatter_dimension=0, tiled=True)  51.7 us
    dot_general x6, matrix products, forward(): jnp.dot(stacked, conv_full, preferred_element_type=jnp.float32) + vectors[0]  50.9 us
  transfers between devices with their start and end apart: 16, of which 11 were waited for; matrix products, arithmetic and copies ran while one was open for 10% of the time, Pallas kernels for 0%

commit v1 on v0

v1 whole, which is shorter than its diff:
```python
import math

import jax
import jax.numpy as jnp
from jax import lax
from jax.sharding import PartitionSpec as P

D = 512
FF = 2048
SECOND_DILATION = 32
SPECIES = 8
STEP = 10


PRECISE = lax.Precision.HIGHEST
NORM_EPSILON = 1e-05
GRAM_EPSILON = 1e-07
ADAM_EPSILON = 1e-08
SCHULZ_LINEAR = 3.4445
SCHULZ_CUBIC = -4.775
SCHULZ_QUINTIC = 2.0315
MUON_MOMENTUM = 0.5
MUON_RATE = 0.1
MUON_DECAY = 0.01
ADAM_RATE = 0.5
ADAM_DECAY = 0.01
BETA_ONE = 0.9
BETA_TWO = 0.95

SWAP = [(0, 1), (1, 0)]


def swap_cores(value):
    return lax.ppermute(value, "section", SWAP)


def flip_bit(value, axis, bit):
    count = lax.axis_size(axis)
    return lax.ppermute(value, axis, [(source, source ^ bit) for source in range(count)])


def bits_of(axis):
    return [1 << power for power in range(int(math.log2(lax.axis_size(axis))))]


def turned(bits, part):
    start = part * len(bits) // 2
    return bits[start:] + bits[:start]


def at(array, index, axis=0):
    return lax.dynamic_index_in_dim(array, index, axis, keepdims=False)


def in_order(core, mine, other, axis=0):
    first = jnp.where(core == 0, mine, other)
    second = jnp.where(core == 0, other, mine)
    return jnp.stack([first, second], axis=axis)


def gather_rows(piece, axis):
    count = lax.axis_size(axis)
    me = lax.axis_index(axis)
    rows = piece.shape[0]
    half = rows // 2
    parts = []
    for part, first in enumerate((0, half)):
        held = {0: lax.slice_in_dim(piece, first, first + half)}
        for bit in turned(bits_of(axis), part):
            keys = sorted(held)
            got = flip_bit(jnp.stack([held[key] for key in keys]), axis, bit)
            for place, key in enumerate(keys):
                held[key ^ bit] = got[place]
        parts.append(held)
    whole = jnp.zeros((count, rows) + piece.shape[1:], piece.dtype)
    for part, first in enumerate((0, half)):
        for key, value in parts[part].items():
            whole = lax.dynamic_update_slice(
                whole, value[None], (me ^ key, first) + (0,) * (piece.ndim - 1)
            )
    return whole


def scatter_sum(chunks, axis):
    me = lax.axis_index(axis)
    count, rows = chunks.shape[:2]
    half = rows // 2
    sums = []
    for part, first in enumerate((0, half)):
        held = {
            key: lax.slice_in_dim(at(chunks, me ^ key), first, first + half)
            for key in range(count)
        }
        for bit in turned(bits_of(axis), part):
            keep = [key for key in sorted(held) if not key & bit]
            sent = jnp.stack([held[key ^ bit].astype(jnp.bfloat16) for key in keep])
            got = flip_bit(sent, axis, bit)
            held = {
                key: held[key] + got[place].astype(jnp.float32) for place, key in enumerate(keep)
            }
        sums.append(held[0])
    return jnp.concatenate(sums)


def sum_along(value, axis):
    me = lax.axis_index(axis)
    count = lax.axis_size(axis)
    rows = value.shape[0] // count
    parts = value.reshape((count, rows) + value.shape[1:])
    total = at(parts, me)
    low = parts.astype(jnp.bfloat16)
    for step in range(1, count):
        moves = [(source, (source + step) % count) for source in range(count)]
        total = total + lax.ppermute(at(low, (me + step) % count), axis, moves).astype(jnp.float32)
    total = total.astype(jnp.bfloat16)
    whole = jnp.zeros((count,) + total.shape, total.dtype)
    whole = lax.dynamic_update_index_in_dim(whole, total, me, 0)
    for step in range(1, count):
        moves = [(source, (source + step) % count) for source in range(count)]
        got = lax.ppermute(total, axis, moves)
        whole = lax.dynamic_update_index_in_dim(whole, got, (me - step) % count, 0)
    return whole.reshape(value.shape)


def sum_whole(value, axes):
    for axis in axes:
        for bit in bits_of(axis):
            value = value + flip_bit(value, axis, bit)
    return value


def sum_halves(value, axis):
    half = value.shape[0] // 2
    halves = []
    for part, first in enumerate((0, half)):
        piece = lax.slice_in_dim(value, first, first + half)
        for bit in turned(bits_of(axis), part):
            piece = piece + flip_bit(piece, axis, bit)
        halves.append(piece)
    return jnp.concatenate(halves)


def gather_weights(core, shard):
    rows = shard.shape[0] // 2
    halves = shard.reshape((2, rows) + shard.shape[1:])
    mine = at(halves, core)
    got = swap_cores(at(halves, 1 - core))
    whole = []
    for block in range(2):
        half = jnp.where(core == block, mine, got)
        full = gather_rows(half, "ns")
        other = swap_cores(full)
        whole.append(in_order(core, full, other, axis=1))
    return whole


def reduce_grad(core, chunks):
    count, rows = chunks.shape[:2]
    halves = chunks.reshape((count, 2, rows // 2) + chunks.shape[2:])
    sent = at(halves, 1 - core, 1).astype(jnp.bfloat16)
    both = at(halves, core, 1) + swap_cores(sent).astype(jnp.float32)
    return sum_along(scatter_sum(both, "ns"), "dp")


def schulz(gram):
    scale = lax.rsqrt(jnp.trace(gram) + GRAM_EPSILON)
    mul = lambda left, right: jnp.dot(
        left, right, precision=PRECISE, preferred_element_type=jnp.float32
    )
    eye = jnp.eye(gram.shape[0], dtype=jnp.float32)
    gram = gram * (scale * scale)
    turn = None
    for sweep_index in range(5):
        square = mul(gram, gram)
        poly = SCHULZ_LINEAR * eye + SCHULZ_CUBIC * gram + SCHULZ_QUINTIC * square
        turn = poly if turn is None else mul(turn, poly)
        if sweep_index < 4:
            gram = mul(gram, mul(poly, poly))
    return turn * scale


def layer_norm(feature_maps, gain_vec, bias_vec):
    average = jnp.mean(feature_maps, axis=-1, keepdims=True)
    centred = feature_maps - average
    variance = jnp.mean(centred * centred, axis=-1, keepdims=True)
    return centred * lax.rsqrt(variance + NORM_EPSILON) * gain_vec + bias_vec


def first_piece(conv_out, values_in, gain_vec, bias_vec):
    return values_in + layer_norm(jax.nn.gelu(conv_out), gain_vec, bias_vec)


def second_piece(branch_out, middle, gain_vec, bias_vec):
    return middle + layer_norm(branch_out, gain_vec, bias_vec)


def spread_taps(masked, tap_spacing):
    win_len = masked.shape[0]
    edge_margin = 4 * SECOND_DILATION
    padded = jnp.pad(masked, ((edge_margin, edge_margin), (0, 0)))
    pieces = [
        lax.slice_in_dim(padded, edge_margin + (tap_index - 4) * tap_spacing, edge_margin + (tap_index - 4) * tap_spacing + win_len)
        for tap_index in range(9)
    ]
    return jnp.concatenate(pieces, axis=1)


def collect_taps(spread_grad, tap_spacing):
    win_len = spread_grad.shape[0]
    feature = spread_grad.shape[1] // 9
    edge_margin = 4 * SECOND_DILATION
    summed = jnp.zeros((win_len, feature), jnp.float32)
    for tap_index in range(9):
        column_block = jnp.pad(
            spread_grad[:, tap_index * feature : (tap_index + 1) * feature],
            ((edge_margin, edge_margin), (0, 0)),
        )
        first = edge_margin - (tap_index - 4) * tap_spacing
        summed = summed + lax.slice_in_dim(column_block, first, first + win_len)
    return summed


def contract_rows(left, right):
    return lax.dot_general(
        left, right, (((0,), (0,)), ((), ())), preferred_element_type=jnp.float32
    )


def contract_cols(left, right):
    return lax.dot_general(
        left, right, (((1,), (1,)), ((), ())), preferred_element_type=jnp.float32
    )


def tall_gram(matrix):
    return lax.dot_general(
        matrix,
        matrix,
        (((0,), (0,)), ((), ())),
        precision=PRECISE,
        preferred_element_type=jnp.float32,
    )


def wide_gram(matrix):
    return lax.dot_general(
        matrix,
        matrix,
        (((1,), (1,)), ((), ())),
        precision=PRECISE,
        preferred_element_type=jnp.float32,
    )


def forward(block_input, padding_mask, tap_spacing, matrices, vectors):
    conv_full, up_full, down_full = matrices
    masked = block_input * padding_mask[:, None].astype(jnp.bfloat16)
    stacked = spread_taps(masked, tap_spacing)
    conv_out = jnp.dot(stacked, conv_full, preferred_element_type=jnp.float32) + vectors[0]
    middle = first_piece(conv_out, block_input.astype(jnp.float32), vectors[1], vectors[2])
    middle_low = middle.astype(jnp.bfloat16)
    hidden_pre = jnp.dot(middle_low, up_full, preferred_element_type=jnp.float32) + vectors[
        3:7
    ].reshape(-1)
    hidden = jax.nn.gelu(hidden_pre).astype(jnp.bfloat16)
    branch_out = jnp.dot(hidden, down_full, preferred_element_type=jnp.float32) + vectors[7]
    block_out = second_piece(branch_out, middle, vectors[8], vectors[9]).astype(jnp.bfloat16)
    return (block_out, (stacked, conv_out, middle, middle_low, hidden_pre, hidden, branch_out))


def backward(context, grad_out, block_input, padding_mask, tap_spacing, matrices, vectors):
    conv_full, up_full, down_full = matrices
    stacked, conv_out, middle, middle_low, hidden_pre, hidden, branch_out = context
    feature = vectors.shape[1]
    unused, pull_two = jax.vjp(second_piece, branch_out, middle, vectors[8], vectors[9])
    d_out, d_middle_res, d_gain_two, d_shift_two = pull_two(grad_out)
    d_out_low = d_out.astype(jnp.bfloat16)
    g_down = contract_rows(hidden, d_out_low)
    d_hidden = contract_cols(d_out_low, down_full)
    unused_pre, pull_gelu = jax.vjp(jax.nn.gelu, hidden_pre)
    (d_pre,) = pull_gelu(d_hidden)
    d_pre_low = d_pre.astype(jnp.bfloat16)
    g_up = contract_rows(middle_low, d_pre_low)
    d_middle = d_middle_res + contract_cols(d_pre_low, up_full)
    unused_conv, pull_one = jax.vjp(
        first_piece, conv_out, block_input.astype(jnp.float32), vectors[1], vectors[2]
    )
    d_conv, d_input_res, d_gain_one, d_shift_one = pull_one(d_middle)
    d_conv_low = d_conv.astype(jnp.bfloat16)
    g_conv = contract_rows(stacked, d_conv_low)
    d_stacked = contract_cols(d_conv_low, conv_full)
    d_input = d_input_res + collect_taps(d_stacked, tap_spacing) * padding_mask[:, None]
    g_vec = jnp.concatenate(
        [
            jnp.sum(d_conv_low, axis=0, dtype=jnp.float32)[None],
            d_gain_one[None],
            d_shift_one[None],
            jnp.sum(d_pre_low, axis=0, dtype=jnp.float32).reshape(4, feature),
            jnp.sum(d_out_low, axis=0, dtype=jnp.float32)[None],
            d_gain_two[None],
            d_shift_two[None],
        ],
        axis=0,
    )
    return (d_input.astype(jnp.bfloat16), (g_conv, g_up, g_down, g_vec))


def on_device(
    inputs,
    cotangent,
    lengths,
    species,
    conv_weight,
    up_weight,
    down_weight,
    conv_moment,
    up_moment,
    down_moment,
    vec_values,
    vec_first,
    vec_second,
    head_weight,
    head_bias,
):
    core = lax.axis_index("section")
    groups = lax.axis_size("ns")
    feature = inputs.shape[2]
    conv_low = conv_weight[0].astype(jnp.bfloat16)
    pair_low = jnp.concatenate(
        [
            up_weight[0].astype(jnp.bfloat16).reshape(-1, feature),
            down_weight[0].astype(jnp.bfloat16),
        ]
    )
    up_rows = up_weight[0].size // feature
    conv_full = gather_weights(core, conv_low)
    pair_full = gather_weights(core, pair_low)
    vectors = in_order(core, vec_values[0], swap_cores(vec_values[0]))
    matrices = []
    for block in range(2):
        pair = pair_full[block].reshape(groups, -1, feature)
        up_parts = pair[:, :up_rows].reshape(groups, feature, -1)
        matrices.append(
            (
                conv_full[block].reshape(-1, feature),
                up_parts.transpose(1, 0, 2).reshape(feature, -1),
                pair[:, up_rows:].reshape(-1, feature),
            )
        )
    batches = inputs.shape[0] // 2
    win_len = inputs.shape[1]
    positions = jnp.arange(win_len)
    species_range = jnp.arange(SPECIES)
    prob_sums = [jnp.zeros((SPECIES, head_weight.shape[1]), jnp.float32)] * 2
    token_counts = jnp.zeros((SPECIES,), jnp.float32)
    gradients = [None, None]
    outputs = [[], []]
    input_grads = [[], []]
    for batch in range(batches):
        window = core * batches + batch
        padding_mask = (positions < at(lengths, window)).astype(jnp.float32)
        species_hit = (species_range == at(species, window)).astype(jnp.float32)
        token_counts = token_counts + species_hit * jnp.sum(padding_mask)
        values = at(inputs, window)
        contexts = []
        for block in range(2):
            block_in = values
            spacing = (1, SECOND_DILATION)[block]
            values, context = forward(
                block_in, padding_mask, spacing, matrices[block], vectors[block]
            )
            logits = jnp.dot(values, head_weight, preferred_element_type=jnp.float32) + head_bias
            chances = jax.nn.softmax(logits, axis=-1)
            weighted = jnp.sum(chances * padding_mask[:, None], axis=0)
            prob_sums[block] = prob_sums[block] + species_hit[:, None] * weighted[None, :]
            outputs[block].append(values)
            contexts.append((block_in, context))
        grad = at(cotangent, window).astype(jnp.float32) * padding_mask[:, None]
        for block in (1, 0):
            block_in, context = contexts[block]
            grad_low, terms = backward(
                context,
                grad,
                block_in,
                padding_mask,
                (1, SECOND_DILATION)[block],
                matrices[block],
                vectors[block],
            )
            input_grads[block].append(grad_low)
            grad = grad_low.astype(jnp.float32)
            if gradients[block] is None:
                gradients[block] = terms
            else:
                gradients[block] = tuple(a + b for a, b in zip(gradients[block], terms))

    def own_windows(parts):
        mine = jnp.stack(parts[0]), jnp.stack(parts[1])
        got = swap_cores(jnp.where(core == 0, mine[1], mine[0]))
        joined = in_order(core, jnp.where(core == 0, mine[0], mine[1]), got)
        return joined.reshape((1, 2 * batches) + joined.shape[2:])

    activations = own_windows(outputs)
    input_grad = own_windows(input_grads)

    reduced = []
    for block in (1, 0):
        g_conv, g_up, g_down, g_vec = gradients[block]
        up_parts = g_up.reshape(feature, groups, -1).transpose(1, 0, 2)
        pair = jnp.concatenate(
            [
                up_parts.reshape(groups, -1, feature),
                g_down.reshape(groups, -1, feature),
            ],
            axis=1,
        )
        conv = reduce_grad(core, g_conv.reshape(groups, -1, feature))
        pair = reduce_grad(core, pair)
        reduced.append((conv, pair))
    reduced.reverse()

    def own_rows(place):
        mine = jnp.where(core == 0, reduced[0][place], reduced[1][place])
        got = swap_cores(jnp.where(core == 0, reduced[1][place], reduced[0][place]))
        joined = in_order(core, mine, got)
        return joined.reshape((-1, feature)).astype(jnp.float32)

    conv_grad = own_rows(0)
    pair_grad = own_rows(1)
    up_grad = pair_grad[:up_rows].reshape(feature, -1)
    down_grad = pair_grad[up_rows:]
    conv_state = MUON_MOMENTUM * conv_moment[0] + conv_grad
    up_state = MUON_MOMENTUM * up_moment[0] + up_grad
    down_state = MUON_MOMENTUM * down_moment[0] + down_grad

    def small_parts(block):
        tail = jnp.concatenate([prob_sums[block].reshape(-1), token_counts])
        tail = jnp.pad(tail, (0, feature - tail.size))
        return jnp.concatenate([gradients[block][3], tail[None]])

    mine, theirs = small_parts(0), small_parts(1)
    small = jnp.where(core == 0, mine, theirs) + swap_cores(jnp.where(core == 0, theirs, mine))
    small = sum_whole(small, ("ns", "dp"))
    vec_grad = small[:-1]
    prob_total = small[-1, : prob_sums[0].size].reshape(prob_sums[0].shape)
    count_total = small[-1, prob_sums[0].size : prob_sums[0].size + SPECIES]

    conv_turn = schulz(sum_halves(tall_gram(conv_state), "ns"))
    up_turn = schulz(sum_halves(wide_gram(up_state), "ns"))
    down_turn = schulz(sum_halves(tall_gram(down_state), "ns"))
    conv_orth = jnp.dot(conv_state, conv_turn, precision=PRECISE)
    up_orth = jnp.dot(up_turn.T, up_state, precision=PRECISE)
    down_orth = jnp.dot(down_state, down_turn, precision=PRECISE)
    keep_factor = 1.0 - MUON_RATE * MUON_DECAY
    conv_next = conv_weight[0] * keep_factor - MUON_RATE * 0.2 * math.sqrt(9 * D) * conv_orth
    up_next = up_weight[0] * keep_factor - MUON_RATE * 0.2 * math.sqrt(FF) * up_orth
    down_next = down_weight[0] * keep_factor - MUON_RATE * 0.2 * math.sqrt(FF) * down_orth
    first_next = BETA_ONE * vec_first[0] + (1.0 - BETA_ONE) * vec_grad
    second_next = BETA_TWO * vec_second[0] + (1.0 - BETA_TWO) * vec_grad * vec_grad
    vec_next = vec_values[0] * (1.0 - ADAM_RATE * ADAM_DECAY) - ADAM_RATE * (
        first_next / (1.0 - BETA_ONE**STEP)
    ) / (jnp.sqrt(second_next / (1.0 - BETA_TWO**STEP)) + ADAM_EPSILON)
    species_freq = prob_total / jnp.maximum(count_total, 1.0)[:, None]
    species_share = SPECIES * count_total / jnp.sum(count_total)
    return (
        activations,
        input_grad,
        conv_grad[None],
        up_grad[None],
        down_grad[None],
        conv_state[None],
        up_state[None],
        down_state[None],
        conv_next[None],
        up_next[None],
        down_next[None],
        conv_next.astype(jnp.bfloat16)[None],
        up_next.astype(jnp.bfloat16)[None],
        down_next.astype(jnp.bfloat16)[None],
        vec_grad[None],
        first_next[None],
        second_next[None],
        vec_next[None],
        species_freq[None],
        species_share[None],
    )


def solution(mesh):
    placed = (
        P(("dp", "ns"), None, None),
        P(("dp", "ns"), None, None),
        P(("dp", "ns")),
        P(("dp", "ns")),
        P("section", "ns", None),
        P("section", None, "ns"),
        P("section", "ns", None),
        P("section", "ns", None),
        P("section", None, "ns"),
        P("section", "ns", None),
        P("section", None, None),
        P("section", None, None),
        P("section", None, None),
        P(),
        P(),
    )
    return jax.shard_map(
        on_device,
        mesh=mesh,
        in_specs=placed,
        out_specs=(
            P("section", ("dp", "ns"), None, None),
            P("section", ("dp", "ns"), None, None),
            P("section", "ns", None),
            P("section", None, "ns"),
            P("section", "ns", None),
            P("section", "ns", None),
            P("section", None, "ns"),
            P("section", "ns", None),
            P("section", "ns", None),
            P("section", None, "ns"),
            P("section", "ns", None),
            P("section", "ns", None),
            P("section", None, "ns"),
            P("section", "ns", None),
            P("section", None, None),
            P("section", None, None),
            P("section", None, None),
            P("section", None, None),
            P("section", None, None),
            P("section", None),
        ),
        check_vma=False,
    )
```

time: 1490 us -> 755 us (0.51)
  waiting for transfers between devices: 745 us -> 147 us
  matrix products: 392 us -> 245 us
  starting transfers between devices: 9.75 us -> 113 us
  blocking collectives: 78.4 us -> 0 us
  between operations: 22.9 us -> 5.86 us
    psum x6 -> x0, waiting for transfers between devices: 486 us -> none  [the longest x5 340 us: on_device(): lax.psum((tall_gram(conv_orth), wide_gram(up_orth), tall_gram(down_orth))...]
    reduce_scatter x3 -> x0, waiting for transfers between devices: 150 us -> none  [the longest x1 98 us: on_device(): lax.psum_scatter(gradients[0], 'ns', scatter_dimension=0, tiled=True)]
    ppermute x4 -> x88, waiting for transfers between devices: 0.01 us -> 147 us  [the longest x48 104 us: flip_bit(): lax.ppermute(value, axis, [(source, source ^ bit) for source in range(cou...]
    all_gather x3 -> x0, waiting for transfers between devices: 109 us -> none  [the longest x1 43.6 us: on_device(): lax.all_gather(conv_weight[0].astype(jnp.bfloat16), 'ns', axis=0, tiled=T...]
    ppermute x4 -> x88, starting transfers between devices: 8.47 us -> 113 us  [the longest x48 61 us: flip_bit(): lax.ppermute(value, axis, [(source, source ^ bit) for source in range(cou...]
    psum x3 -> x0, blocking collectives: 78.4 us -> none  [the longest x1 40.9 us: on_device(): prob_total, count_total = lax.psum((prob_sums, token_counts), ('dp', 'ns'))]
    unnamed x376 -> x179, local copies, waits for them, and re-layouts: 90.6 us -> 37 us
    dot_general x6 -> x2, matrix products: 46.2 us -> 4.87 us  [forward(): jnp.dot(hidden, down_full, preferred_element_type=jnp.float32) + vectors[7]]
  transfers between devices with their start and end apart: 16 -> 88, of which waited for: 11 -> 31; matrix products, arithmetic and copies ran while one was open for 10% -> 32% of each run, Pallas kernels for 0% -> 0%
where the time goes in v1:
time: 755 us; the launch traced here: 745 us
  matrix products  245 us (32%)
  waiting for transfers between devices  147 us (19%)
  local copies, waits for them, and re-layouts  127 us (17%)
  starting transfers between devices  113 us (15%)
  other arithmetic  108 us (14%)
    ppermute x48, waiting for transfers between devices, flip_bit(): lax.ppermute(value, axis, [(source, source ^ bit) for source in range(cou...  104 us
    dot_general x51, matrix products, schulz(): jnp.dot(left, right, precision=PRECISE, preferred_element_type=jnp.float32)  102 us
    ppermute x48, starting transfers between devices, flip_bit(): lax.ppermute(value, axis, [(source, source ^ bit) for source in range(cou...  61 us
    dot_general x6, matrix products, contract_cols(): lax.dot_general(left, right, (((1,), (1,)), ((), ())), preferred_element_...  45.3 us
    dot_general x6, matrix products, contract_rows(): lax.dot_general(left, right, (((0,), (0,)), ((), ())), preferred_element_...  41.7 us
    unnamed x179, local copies, waits for them, and re-layouts  37 us
    ppermute x12, starting transfers between devices, sum_along(): got = lax.ppermute(total, axis, moves)  29.2 us
    ppermute x12, waiting for transfers between devices, sum_along(): lax.ppermute(at(low, (me + step) % count), axis, moves).astype(jnp.float32)  24.3 us
  transfers between devices with their start and end apart: 88, of which 31 were waited for; matrix products, arithmetic and copies ran while one was open for 32% of the time, Pallas kernels for 0%

profile of v1, /device:TPU:0, one launch (start us, length us, event | category | flops | bytes accessed | tf_op | source)
XLA Modules:
  0.0 744.6 jit_solution(11227233099913076584)
XLA Ops:
  20.0 3.6 copy-done.46
  49.9 4.8 collective-permute-done.13
  62.0 18.0 %collective-permute-done.19 = bf16[2,256,512]{2,1,0:T(8,128)(2,1)S(1)} collective-permute-done((bf16[2,256,512]{2,1,0:T(8,128)(2,1)S(1)}, bf16[2,256,512]{2,1,0:T(8,128)(2,1)S(1)}, u32[]{:S(2)}, u32[]{:S(2)}) %collective-permute-start.19) | collective-permute-done | bytes 524320 | tf_op jit(solution)/shard_map/ppermute | solution.py:39
  88.6 16.0 %collective-permute-done.14 = bf16[2,288,512]{2,1,0:T(8,128)(2,1)S(1)} collective-permute-done((bf16[2,288,512]{2,1,0:T(8,128)(2,1)S(1)}, bf16[2,288,512]{2,1,0:T(8,128)(2,1)S(1)}, u32[]{:S(2)}, u32[]{:S(2)}) %collective-permute-start.14) | collective-permute-done | bytes 589856 | tf_op jit(solution)/shard_map/ppermute | solution.py:39
  117.3 4.3 copy.172
  127.0 4.1 copy.169
  137.9 9.9 %fusion.191 = (f32[1024]{0:T(1024)S(1)}, f32[1024,512]{0,1:T(8,128)S(1)}) fusion(f32[512]{0:T(512)S(1)} %bitcast.586, bf16[1024,4608]{0,1:T(8,128)(2,1)} %copy-done.46, bf16[4608,512]{1,0:T(8,128)(2,1)S(1)} %bitcast.552), kind=kOutput, calls=%fused_computation.551 | convolution fusion | flops 4837080064 | bytes 16259072 | tf_op jit(solution)/shard_map/dot_general | solution.py:259
  150.2 7.6 %multiply_convert_fusion.1 = (bf16[1024,2048]{1,0:T(8,128)(2,1)S(1)}, f32[1024,2048]{1,0:T(8,128)}) fusion(f32[2048]{0:T(1024)S(1)} %bitcast.642, bf16[512,2048]{0,1:T(8,128)(2,1)S(1)} %bitcast.568, f32[512]{0:T(512)S(1)} %bitcast.636, f32[512]{0:T(512)S(1)} %bitcast.615, f32[1024]{0:T(1024)S(1)} %fusion.177, f32[1024]{0:T(1024)S(1)} %broadcast_multiply_fusion.6, ...), kind=kOutput, calls=%fused_computation.23 | convolution fusion | flops 2176843776 | bytes 17848320 | tf_op jit(solution)/shard_map/dot_general | solution.py:262
  167.8 3.6 copy-done.47
  171.4 8.2 %fusion.192 = (f32[1024]{0:T(1024)S(1)}, f32[1024,512]{0,1:T(8,128)S(1)}) fusion(f32[512]{0:T(512)S(1)} %bitcast.603, bf16[1024,4608]{0,1:T(8,128)(2,1)} %copy-done.47, bf16[4608,512]{1,0:T(8,128)(2,1)S(1)} %bitcast.556), kind=kOutput, calls=%fused_computation.552 | convolution fusion | flops 4837080064 | bytes 16259072 | tf_op jit(solution)/shard_map/dot_general | solution.py:259
  181.1 7.8 %multiply_convert_fusion = (bf16[1024,2048]{1,0:T(8,128)(2,1)S(1)}, f32[1024,2048]{1,0:T(8,128)}) fusion(f32[2048]{0:T(1024)S(1)} %bitcast.644, bf16[512,2048]{0,1:T(8,128)(2,1)S(1)} %bitcast.570, f32[512]{0:T(512)S(1)} %bitcast.648, f32[512]{0:T(512)S(1)} %bitcast.622, f32[1024]{0:T(1024)S(1)} %fusion.179, f32[1024]{0:T(1024)S(1)} %broadcast_multiply_fusion.4, ...), kind=kOutput, calls=%fused_computation.22 | convolution fusion | flops 2176843776 | bytes 17848320 | tf_op jit(solution)/shard_map/dot_general | solution.py:262
  195.7 4.4 fusion.222
  200.1 9.8 %convert_reduce_fusion = (f32[2048]{0:T(1024)S(1)}, bf16[1024,2048]{1,0:T(8,128)(2,1)S(1)}) fusion(f32[1024,2048]{1,0:T(8,128)} %get-tuple-element.283, f32[2048]{0:T(1024)S(1)} %bitcast.645, bf16[1024,512]{0,1:T(8,128)(2,1)S(1)} %get-tuple-element.127, bf16[2048,512]{1,0:T(8,128)(2,1)S(1)} %bitcast.577), kind=kOutput, calls=%fused_computation.20 | convolution fusion | flops 2195716096 | bytes 15745024 | tf_op jit(solution)/shard_map/dot_general | solution.py:230
  210.0 3.5 fusion.194
  213.5 5.2 fusion.151
  223.4 11.3 %fusion.220 = f32[4608,512]{1,0:T(8,128)} fusion(bf16[1024,4608]{0,1:T(8,128)(2,1)} %copy-done.47, bf16[1024,512]{0,1:T(8,128)(2,1)S(1)} %get-tuple-element.129), kind=kOutput, calls=%fused_computation.571 | convolution fusion | flops 4831838208 | bytes 19922944 | tf_op jit(solution)/shard_map/dot_general | solution.py:224
  234.6 9.1 %fusion.253 = f32[1024,4608]{0,1:T(8,128)} fusion(bf16[4608,512]{1,0:T(8,128)(2,1)S(1)} %bitcast.557, bf16[1024,512]{0,1:T(8,128)(2,1)S(1)} %get-tuple-element.129), kind=kOutput, calls=%fused_computation.604 | convolution fusion | flops 4831838208 | bytes 24641536 | tf_op jit(solution)/shard_map/dot_general | solution.py:230
  243.7 9.3 %fusion.205 = (f32[1024,512]{0,1:T(8,128)S(1)}, f32[1024,512]{0,1:T(8,128)S(1)}, f32[1024,512]{0,1:T(8,128)S(1)}, f32[1024,512]{0,1:T(8,128)S(1)}, f32[1024,512]...) fusion(f32[1024,4608]{0,1:T(8,128)} %fusion.253), kind=kLoop, calls=%fused_computation.556 | loop fusion | bytes 33554432 | tf_op jit(solution)/shard_map/slice | solution.py:215
  253.0 6.5 convert_reduce_fusion.2
  262.9 4.3 fusion.221
  267.3 10.0 %convert_reduce_fusion.1 = (f32[2048]{0:T(1024)S(1)}, bf16[1024,2048]{1,0:T(8,128)(2,1)S(1)}) fusion(f32[1024,2048]{1,0:T(8,128)} %get-tuple-element.277, f32[2048]{0:T(1024)S(1)} %bitcast.643, bf16[1024,512]{0,1:T(8,128)(2,1)S(1)} %get-tuple-element.123, bf16[2048,512]{1,0:T(8,128)(2,1)S(1)} %bitcast.575), kind=kOutput, calls=%fused_computation.21 | convolution fusion | flops 2195716096 | bytes 15745024 | tf_op jit(solution)/shard_map/dot_general | solution.py:230
  277.3 3.4 fusion.193
  280.8 5.1 fusion.155
  290.4 11.4 %fusion.219 = f32[4608,512]{1,0:T(8,128)} fusion(bf16[1024,4608]{0,1:T(8,128)(2,1)} %copy-done.46, bf16[1024,512]{0,1:T(8,128)(2,1)S(1)} %get-tuple-element.125), kind=kOutput, calls=%fused_computation.570 | convolution fusion | flops 4831838208 | bytes 19922944 | tf_op jit(solution)/shard_map/dot_general | solution.py:224
  301.8 9.5 %fusion.254 = f32[1024,4608]{0,1:T(8,128)} fusion(bf16[4608,512]{1,0:T(8,128)(2,1)S(1)} %bitcast.555, bf16[1024,512]{0,1:T(8,128)(2,1)S(1)} %get-tuple-element.125), kind=kOutput, calls=%fused_computation.605 | convolution fusion | flops 4831838208 | bytes 24641536 | tf_op jit(solution)/shard_map/dot_general | solution.py:230
  311.4 3.6 select_bitcast_fusion.9
  315.0 4.9 copy.232
  321.6 4.4 pad_maximum_fusion.1
  326.1 3.3 copy-done.3
  331.1 4.0 fusion.18
  335.6 4.8 copy.233
  340.6 4.4 pad_maximum_fusion
  350.9 10.1 %fusion.204 = (f32[1024,512]{0,1:T(8,128)S(1)}, f32[1024,512]{0,1:T(8,128)S(1)}, f32[1024,512]{0,1:T(8,128)S(1)}, f32[1024,512]{0,1:T(8,128)S(1)}, f32[1024,512]...) fusion(f32[1024,4608]{0,1:T(8,128)} %fusion.254), kind=kLoop, calls=%fused_computation.555 | loop fusion | bytes 33554432 | tf_op jit(solution)/shard_map/slice | solution.py:215
  362.7 8.4 %select_bitcast_fusion.8 = (bf16[1,1024,512]{1,2,0:T(8,128)(2,1)}, bf16[1024,512]{0,1:T(8,128)(2,1)}) fusion(bf16[1024,512]{0,1:T(8,128)(2,1)S(1)} %get-tuple-element.144, pred[]{:T(512)S(6)} %eq.114, f32[1024,512]{0,1:T(8,128)S(1)} %get-tuple-element.287, f32[1024]{0:T(1024)S(1)} %get-tuple-element.298, f32[1024,512]{0,1:T(8,128)} %get-tuple-element.156, ...), kind=kLoop, calls=%fused_computation.283 | loop fusion | flops 6291456 | bytes 24121344 | tf_op jit(solution)/shard_map/jit(_where)/select_n | solution.py:399
  373.7 4.2 fusion.17
  392.7 3.5 bitcast_add_fusion.2
  398.6 4.0 bitcast_add_fusion.3
  409.0 3.8 bitcast_add_fusion.1
  414.4 8.9 %collective-permute-done.49 = bf16[2,256,512]{2,1,0:T(8,128)(2,1)S(1)} collective-permute-done((bf16[2,256,512]{2,1,0:T(8,128)(2,1)S(1)}, bf16[2,256,512]{2,1,0:T(8,128)(2,1)S(1)}, u32[]{:S(2)}, u32[]{:S(2)}) %collective-permute-start.49) | collective-permute-done | bytes 524320 | tf_op jit(solution)/shard_map/ppermute | solution.py:39
  430.4 3.4 collective-permute-done.50
  437.4 11.1 %collective-permute-done.26 = bf16[2,288,512]{2,1,0:T(8,128)(2,1)S(1)} collective-permute-done((bf16[2,288,512]{2,1,0:T(8,128)(2,1)S(1)}, bf16[2,288,512]{2,1,0:T(8,128)(2,1)S(1)}, u32[]{:S(2)}, u32[]{:S(2)}) %collective-permute-start.26) | collective-permute-done | bytes 589856 | tf_op jit(solution)/shard_map/ppermute | solution.py:39
  450.1 4.0 collective-permute-done.63
  458.9 3.4 collective-permute-start.66
  462.3 3.1 collective-permute-done.38
  466.8 3.6 collective-permute-done.27
  477.9 4.5 collective-permute-start.68
  482.7 5.8 collective-permute-done.54
  490.1 3.6 collective-permute-start.56
  493.7 3.3 collective-permute-done.56
  497.0 3.6 collective-permute-start.57
  501.2 5.3 collective-permute-done.57
  515.9 5.7 collective-permute-start.32
  521.6 6.8 collective-permute-done.42
  528.7 7.9 %collective-permute-start.44 = (bf16[144,512]{1,0:T(8,128)(2,1)S(1)}, bf16[144,512]{1,0:T(8,128)(2,1)S(1)}, u32[]{:S(2)}, u32[]{:S(2)}) collective-permute-start(bf16[144,512]{1,0:T(8,128)(2,1)S(1)} %get-tuple-element.141), channel_id=1, source_target_pairs={{0,4},{4,8},{8,12},{12,0},{1,5},{5,9},{9,13},{13,1},{2,6},{6,10},{... | collective-permute-start | bytes 442376 | tf_op jit(solution)/shard_map/ppermute | solution.py:120
  536.6 7.5 %collective-permute-done.31 = bf16[144,512]{1,0:T(8,128)(2,1)S(1)} collective-permute-done((bf16[144,512]{1,0:T(8,128)(2,1)S(1)}, bf16[144,512]{1,0:T(8,128)(2,1)S(1)}, u32[]{:S(2)}, u32[]{:S(2)}) %collective-permute-start.31) | collective-permute-done | bytes 147488 | tf_op jit(solution)/shard_map/ppermute | solution.py:114
  544.3 8.1 %collective-permute-start.33 = (bf16[144,512]{1,0:T(8,128)(2,1)S(1)}, bf16[144,512]{1,0:T(8,128)(2,1)S(1)}, u32[]{:S(2)}, u32[]{:S(2)}) collective-permute-start(bf16[144,512]{1,0:T(8,128)(2,1)S(1)} %get-tuple-element.139), channel_id=1, source_target_pairs={{0,4},{4,8},{8,12},{12,0},{1,5},{5,9},{9,13},{13,1},{2,6},{6,10},{... | collective-permute-start | bytes 442376 | tf_op jit(solution)/shard_map/ppermute | solution.py:120
  556.0 3.9 collective-permute-done.34
  578.0 4.4 fusion.19
  586.8 6.8 collective-permute-done.79
  599.1 5.8 collective-permute-done.71
  610.2 8.0 %collective-permute-done.76 = f32[256,512]{1,0:T(8,128)S(1)} collective-permute-done((f32[256,512]{1,0:T(8,128)S(1)}, f32[256,512]{1,0:T(8,128)S(1)}, u32[]{:S(2)}, u32[]{:S(2)}) %collective-permute-start.76) | collective-permute-done | bytes 524320 | tf_op jit(solution)/shard_map/ppermute | solution.py:39
  623.9 3.1 fusion.116
  640.0 4.3 fusion.74
  738.6 4.0 fusion.14
  (622 shorter events, 344.6 us)
Async XLA Ops:
  1.4 25.6 %collective-permute-start.6 = (f32[10,512]{1,0:T(8,128)S(1)}, f32[10,512]{1,0:T(8,128)S(1)}, u32[]{:S(2)}, u32[]{:S(2)}) collective-permute-start(f32[10,512]{1,0:T(8,128)S(1)} %bitcast.621), channel_id=1, source_target_pairs={{0,16},{16,0},{1,17},{17,1},{2,18},{18,2},{3,19},{19,3},{4,20},{20... | collective-permute-start | bytes 61448 | tf_op jit(solution)/shard_map/ppermute | solution.py:34
  4.8 22.9 %collective-permute-start.7 = (bf16[512,512]{1,0:T(8,128)(2,1)}, bf16[512,512]{1,0:T(8,128)(2,1)}, u32[]{:S(2)}, u32[]{:S(2)}) collective-permute-start(bf16[512,512]{1,0:T(8,128)(2,1)} %dynamic-slice_bitcast_fusion.1), channel_id=1, source_target_pairs={{0,16},{16,0},{1,17},{17,1},{2,18},{18,2},{3,19},{19,3},{4,20},{20... | collective-permute-start | bytes 1572872 | tf_op jit(solution)/shard_map/ppermute | solution.py:34
  6.8 29.9 %collective-permute-start = (bf16[576,512]{1,0:T(8,128)(2,1)}, bf16[576,512]{1,0:T(8,128)(2,1)}, u32[]{:S(2)}, u32[]{:S(2)}) collective-permute-start(bf16[576,512]{1,0:T(8,128)(2,1)} %dynamic-slice_bitcast_fusion), channel_id=1, source_target_pairs={{0,16},{16,0},{1,17},{17,1},{2,18},{18,2},{3,19},{19,3},{4,20},{20... | collective-permute-start | bytes 1769480 | tf_op jit(solution)/shard_map/ppermute | solution.py:34
  29.1 15.6 %collective-permute-start.20 = (bf16[1,256,512]{2,1,0:T(8,128)(2,1)S(1)}, bf16[1,256,512]{2,1,0:T(8,128)(2,1)S(1)}, u32[]{:S(2)}, u32[]{:S(2)}) collective-permute-start(bf16[1,256,512]{2,1,0:T(8,128)(2,1)S(1)} %get-tuple-element.247), channel_id=1, source_target_pairs={{0,2},{1,3},{2,0},{3,1},{4,6},{5,7},{6,4},{7,5},{8,10},{9,11},{10,... | collective-permute-start | bytes 786440 | tf_op jit(solution)/shard_map/ppermute | solution.py:39
  32.1 14.1 %collective-permute-start.18 = (bf16[1,256,512]{2,1,0:T(8,128)(2,1)S(1)}, bf16[1,256,512]{2,1,0:T(8,128)(2,1)S(1)}, u32[]{:S(2)}, u32[]{:S(2)}) collective-permute-start(bf16[1,256,512]{2,1,0:T(8,128)(2,1)S(1)} %get-tuple-element.248), channel_id=1, source_target_pairs={{0,1},{1,0},{2,3},{3,2},{4,5},{5,4},{6,7},{7,6},{8,9},{9,8},{10,11... | collective-permute-start | bytes 786440 | tf_op jit(solution)/shard_map/ppermute | solution.py:39
  33.6 14.3 %collective-permute-start.10 = (bf16[1,256,512]{2,1,0:T(8,128)(2,1)S(1)}, bf16[1,256,512]{2,1,0:T(8,128)(2,1)S(1)}, u32[]{:S(2)}, u32[]{:S(2)}) collective-permute-start(bf16[1,256,512]{2,1,0:T(8,128)(2,1)S(1)} %get-tuple-element.249), channel_id=1, source_target_pairs={{0,2},{1,3},{2,0},{3,1},{4,6},{5,7},{6,4},{7,5},{8,10},{9,11},{10,... | collective-permute-start | bytes 786440 | tf_op jit(solution)/shard_map/ppermute | solution.py:39
  38.0 22.8 %collective-permute-start.15 = (bf16[1,288,512]{2,1,0:T(8,128)(2,1)S(1)}, bf16[1,288,512]{2,1,0:T(8,128)(2,1)S(1)}, u32[]{:S(2)}, u32[]{:S(2)}) collective-permute-start(bf16[1,288,512]{2,1,0:T(8,128)(2,1)S(1)} %get-tuple-element.233), channel_id=1, source_target_pairs={{0,2},{1,3},{2,0},{3,1},{4,6},{5,7},{6,4},{7,5},{8,10},{9,11},{10,... | collective-permute-start | bytes 884744 | tf_op jit(solution)/shard_map/ppermute | solution.py:39
  46.2 15.2 %collective-permute-start.3 = (bf16[1,288,512]{2,1,0:T(8,128)(2,1)S(1)}, bf16[1,288,512]{2,1,0:T(8,128)(2,1)S(1)}, u32[]{:S(2)}, u32[]{:S(2)}) collective-permute-start(bf16[1,288,512]{2,1,0:T(8,128)(2,1)S(1)} %get-tuple-element.235), channel_id=1, source_target_pairs={{0,2},{1,3},{2,0},{3,1},{4,6},{5,7},{6,4},{7,5},{8,10},{9,11},{10,... | collective-permute-start | bytes 884744 | tf_op jit(solution)/shard_map/ppermute | solution.py:39
  47.9 34.1 %collective-permute-start.9 = (bf16[2,256,512]{2,1,0:T(8,128)(2,1)S(1)}, bf16[2,256,512]{2,1,0:T(8,128)(2,1)S(1)}, u32[]{:S(2)}, u32[]{:S(2)}) collective-permute-start(bf16[2,256,512]{2,1,0:T(8,128)(2,1)S(1)} %pad_maximum_fusion.28), channel_id=1, source_target_pairs={{0,2},{1,3},{2,0},{3,1},{4,6},{5,7},{6,4},{7,5},{8,10},{9,11},{10,... | collective-permute-start | bytes 1572872 | tf_op jit(solution)/shard_map/ppermute | solution.py:39
  54.6 25.3 %collective-permute-start.19 = (bf16[2,256,512]{2,1,0:T(8,128)(2,1)S(1)}, bf16[2,256,512]{2,1,0:T(8,128)(2,1)S(1)}, u32[]{:S(2)}, u32[]{:S(2)}) collective-permute-start(bf16[2,256,512]{2,1,0:T(8,128)(2,1)S(1)} %pad_maximum_fusion.30), channel_id=1, source_target_pairs={{0,2},{1,3},{2,0},{3,1},{4,6},{5,7},{6,4},{7,5},{8,10},{9,11},{10,... | collective-permute-start | bytes 1572872 | tf_op jit(solution)/shard_map/ppermute | solution.py:39
  58.5 28.6 %collective-permute-start.11 = (bf16[2,256,512]{2,1,0:T(8,128)(2,1)S(1)}, bf16[2,256,512]{2,1,0:T(8,128)(2,1)S(1)}, u32[]{:S(2)}, u32[]{:S(2)}) collective-permute-start(bf16[2,256,512]{2,1,0:T(8,128)(2,1)S(1)} %pad_maximum_fusion.29), channel_id=1, source_target_pairs={{0,1},{1,0},{2,3},{3,2},{4,5},{5,4},{6,7},{7,6},{8,9},{9,8},{10,11... | collective-permute-start | bytes 1572872 | tf_op jit(solution)/shard_map/ppermute | solution.py:39
  60.8 25.0 %collective-permute-start.21 = (bf16[2,256,512]{2,1,0:T(8,128)(2,1)S(1)}, bf16[2,256,512]{2,1,0:T(8,128)(2,1)S(1)}, u32[]{:S(2)}, u32[]{:S(2)}) collective-permute-start(bf16[2,256,512]{2,1,0:T(8,128)(2,1)S(1)} %pad_maximum_fusion.31), channel_id=1, source_target_pairs={{0,1},{1,0},{2,3},{3,2},{4,5},{5,4},{6,7},{7,6},{8,9},{9,8},{10,11... | collective-permute-start | bytes 1572872 | tf_op jit(solution)/shard_map/ppermute | solution.py:39
  61.5 48.0 %collective-permute-start.2 = (bf16[2,288,512]{2,1,0:T(8,128)(2,1)S(1)}, bf16[2,288,512]{2,1,0:T(8,128)(2,1)S(1)}, u32[]{:S(2)}, u32[]{:S(2)}) collective-permute-start(bf16[2,288,512]{2,1,0:T(8,128)(2,1)S(1)} %pad_maximum_fusion.20), channel_id=1, source_target_pairs={{0,2},{1,3},{2,0},{3,1},{4,6},{5,7},{6,4},{7,5},{8,10},{9,11},{10,... | collective-permute-start | bytes 1769480 | tf_op jit(solution)/shard_map/ppermute | solution.py:39
  79.9 32.5 %collective-permute-start.4 = (bf16[2,288,512]{2,1,0:T(8,128)(2,1)S(1)}, bf16[2,288,512]{2,1,0:T(8,128)(2,1)S(1)}, u32[]{:S(2)}, u32[]{:S(2)}) collective-permute-start(bf16[2,288,512]{2,1,0:T(8,128)(2,1)S(1)} %pad_maximum_fusion.21), channel_id=1, source_target_pairs={{0,1},{1,0},{2,3},{3,2},{4,5},{5,4},{6,7},{7,6},{8,9},{9,8},{10,11... | collective-permute-start | bytes 1769480 | tf_op jit(solution)/shard_map/ppermute | solution.py:39
  82.1 22.5 %collective-permute-start.14 = (bf16[2,288,512]{2,1,0:T(8,128)(2,1)S(1)}, bf16[2,288,512]{2,1,0:T(8,128)(2,1)S(1)}, u32[]{:S(2)}, u32[]{:S(2)}) collective-permute-start(bf16[2,288,512]{2,1,0:T(8,128)(2,1)S(1)} %pad_maximum_fusion.22), channel_id=1, source_target_pairs={{0,2},{1,3},{2,0},{3,1},{4,6},{5,7},{6,4},{7,5},{8,10},{9,11},{10,... | collective-permute-start | bytes 1769480 | tf_op jit(solution)/shard_map/ppermute | solution.py:39
  85.8 21.7 %collective-permute-start.16 = (bf16[2,288,512]{2,1,0:T(8,128)(2,1)S(1)}, bf16[2,288,512]{2,1,0:T(8,128)(2,1)S(1)}, u32[]{:S(2)}, u32[]{:S(2)}) collective-permute-start(bf16[2,288,512]{2,1,0:T(8,128)(2,1)S(1)} %pad_maximum_fusion.23), channel_id=1, source_target_pairs={{0,1},{1,0},{2,3},{3,2},{4,5},{5,4},{6,7},{7,6},{8,9},{9,8},{10,11... | collective-permute-start | bytes 1769480 | tf_op jit(solution)/shard_map/ppermute | solution.py:39
  87.2 26.7 %collective-permute-start.22 = (bf16[4,512,512]{2,1,0:T(8,128)(2,1)S(1)}, bf16[4,512,512]{2,1,0:T(8,128)(2,1)S(1)}, u32[]{:S(2)}, u32[]{:S(2)}) collective-permute-start(bf16[4,512,512]{2,1,0:T(8,128)(2,1)S(1)} %slice_dynamic-update-slice_fusion.8), channel_id=1, source_target_pairs={{0,16},{16,0},{1,17},{17,1},{2,18},{18,2},{3,19},{19,3},{4,20},{20... | collective-permute-start | bytes 6291464 | tf_op jit(solution)/shard_map/ppermute | solution.py:34
  104.6 17.0 %collective-permute-start.12 = (bf16[4,512,512]{2,1,0:T(8,128)(2,1)}, bf16[4,512,512]{2,1,0:T(8,128)(2,1)}, u32[]{:S(2)}, u32[]{:S(2)}) collective-permute-start(bf16[4,512,512]{2,1,0:T(8,128)(2,1)} %slice_dynamic-update-slice_fusion.12), channel_id=1, source_target_pairs={{0,16},{16,0},{1,17},{17,1},{2,18},{18,2},{3,19},{19,3},{4,20},{20... | collective-permute-start | bytes 6291464 | tf_op jit(solution)/shard_map/ppermute | solution.py:34
  109.0 22.1 %collective-permute-start.17 = (bf16[4,576,512]{2,1,0:T(8,128)(2,1)}, bf16[4,576,512]{2,1,0:T(8,128)(2,1)}, u32[]{:S(2)}, u32[]{:S(2)}) collective-permute-start(bf16[4,576,512]{2,1,0:T(8,128)(2,1)} %slice_dynamic-update-slice_fusion), channel_id=1, source_target_pairs={{0,16},{16,0},{1,17},{17,1},{2,18},{18,2},{3,19},{19,3},{4,20},{20... | collective-permute-start | bytes 7077896 | tf_op jit(solution)/shard_map/ppermute | solution.py:34
  113.9 20.9 %collective-permute-start.5 = (bf16[4,576,512]{2,1,0:T(8,128)(2,1)}, bf16[4,576,512]{2,1,0:T(8,128)(2,1)}, u32[]{:S(2)}, u32[]{:S(2)}) collective-permute-start(bf16[4,576,512]{2,1,0:T(8,128)(2,1)} %slice_dynamic-update-slice_fusion.4), channel_id=1, source_target_pairs={{0,16},{16,0},{1,17},{17,1},{2,18},{18,2},{3,19},{19,3},{4,20},{20... | collective-permute-start | bytes 7077896 | tf_op jit(solution)/shard_map/ppermute | solution.py:34
  321.1 62.2 %collective-permute-start.23 = (bf16[1,1024,512]{1,2,0:T(8,128)(2,1)}, bf16[1,1024,512]{1,2,0:T(8,128)(2,1)}, u32[]{:S(2)}, u32[]{:S(2)}) collective-permute-start(bf16[1,1024,512]{1,2,0:T(8,128)(2,1)} %get-tuple-element.145), channel_id=1, source_target_pairs={{0,16},{16,0},{1,17},{17,1},{2,18},{18,2},{3,19},{19,3},{4,20},{20... | collective-permute-start | bytes 3145736 | tf_op jit(solution)/shard_map/ppermute | solution.py:34
  331.0 61.6 %collective-permute-start.59 = (bf16[4,512,512]{2,1,0:T(8,128)(2,1)}, bf16[4,512,512]{2,1,0:T(8,128)(2,1)}, u32[]{:S(2)}, u32[]{:S(2)}) collective-permute-start(bf16[4,512,512]{2,1,0:T(8,128)(2,1)} %fusion.60), channel_id=1, source_target_pairs={{0,16},{16,0},{1,17},{17,1},{2,18},{18,2},{3,19},{19,3},{4,20},{20... | collective-permute-start | bytes 6291464 | tf_op jit(solution)/shard_map/ppermute | solution.py:34
  335.1 68.9 %collective-permute-start.36 = (bf16[4,576,512]{2,1,0:T(8,128)(2,1)}, bf16[4,576,512]{2,1,0:T(8,128)(2,1)}, u32[]{:S(2)}, u32[]{:S(2)}) collective-permute-start(bf16[4,576,512]{2,1,0:T(8,128)(2,1)} %fusion.18), channel_id=1, source_target_pairs={{0,16},{16,0},{1,17},{17,1},{2,18},{18,2},{3,19},{19,3},{4,20},{20... | collective-permute-start | bytes 7077896 | tf_op jit(solution)/shard_map/ppermute | solution.py:34
  348.9 49.7 %collective-permute-start.48 = (bf16[4,512,512]{2,1,0:T(8,128)(2,1)}, bf16[4,512,512]{2,1,0:T(8,128)(2,1)}, u32[]{:S(2)}, u32[]{:S(2)}) collective-permute-start(bf16[4,512,512]{2,1,0:T(8,128)(2,1)} %fusion.59), channel_id=1, source_target_pairs={{0,16},{16,0},{1,17},{17,1},{2,18},{18,2},{3,19},{19,3},{4,20},{20... | collective-permute-start | bytes 6291464 | tf_op jit(solution)/shard_map/ppermute | solution.py:34
  383.2 24.5 %collective-permute-start.25 = (bf16[4,576,512]{2,1,0:T(8,128)(2,1)}, bf16[4,576,512]{2,1,0:T(8,128)(2,1)}, u32[]{:S(2)}, u32[]{:S(2)}) collective-permute-start(bf16[4,576,512]{2,1,0:T(8,128)(2,1)} %fusion.17), channel_id=1, source_target_pairs={{0,16},{16,0},{1,17},{17,1},{2,18},{18,2},{3,19},{19,3},{4,20},{20... | collective-permute-start | bytes 7077896 | tf_op jit(solution)/shard_map/ppermute | solution.py:34
  396.4 28.5 %collective-permute-start.62 = (bf16[2,256,512]{2,1,0:T(8,128)(2,1)S(1)}, bf16[2,256,512]{2,1,0:T(8,128)(2,1)S(1)}, u32[]{:S(2)}, u32[]{:S(2)}) collective-permute-start(bf16[2,256,512]{2,1,0:T(8,128)(2,1)S(1)} %pad_maximum_fusion.35), channel_id=1, source_target_pairs={{0,2},{1,3},{2,0},{3,1},{4,6},{5,7},{6,4},{7,5},{8,10},{9,11},{10,... | collective-permute-start | bytes 1572872 | tf_op jit(solution)/shard_map/ppermute | solution.py:39
  397.1 16.1 %collective-permute-start.60 = (bf16[2,256,512]{2,1,0:T(8,128)(2,1)S(1)}, bf16[2,256,512]{2,1,0:T(8,128)(2,1)S(1)}, u32[]{:S(2)}, u32[]{:S(2)}) collective-permute-start(bf16[2,256,512]{2,1,0:T(8,128)(2,1)S(1)} %pad_maximum_fusion.34), channel_id=1, source_target_pairs={{0,1},{1,0},{2,3},{3,2},{4,5},{5,4},{6,7},{7,6},{8,9},{9,8},{10,11... | collective-permute-start | bytes 1572872 | tf_op jit(solution)/shard_map/ppermute | solution.py:39
  402.9 26.9 %collective-permute-start.51 = (bf16[2,256,512]{2,1,0:T(8,128)(2,1)S(1)}, bf16[2,256,512]{2,1,0:T(8,128)(2,1)S(1)}, u32[]{:S(2)}, u32[]{:S(2)}) collective-permute-start(bf16[2,256,512]{2,1,0:T(8,128)(2,1)S(1)} %pad_maximum_fusion.33), channel_id=1, source_target_pairs={{0,2},{1,3},{2,0},{3,1},{4,6},{5,7},{6,4},{7,5},{8,10},{9,11},{10,... | collective-permute-start | bytes 1572872 | tf_op jit(solution)/shard_map/ppermute | solution.py:39
  404.0 19.2 %collective-permute-start.49 = (bf16[2,256,512]{2,1,0:T(8,128)(2,1)S(1)}, bf16[2,256,512]{2,1,0:T(8,128)(2,1)S(1)}, u32[]{:S(2)}, u32[]{:S(2)}) collective-permute-start(bf16[2,256,512]{2,1,0:T(8,128)(2,1)S(1)} %pad_maximum_fusion.32), channel_id=1, source_target_pairs={{0,1},{1,0},{2,3},{3,2},{4,5},{5,4},{6,7},{7,6},{8,9},{9,8},{10,11... | collective-permute-start | bytes 1572872 | tf_op jit(solution)/shard_map/ppermute | solution.py:39
  407.8 28.1 %collective-permute-start.37 = (bf16[2,288,512]{2,1,0:T(8,128)(2,1)S(1)}, bf16[2,288,512]{2,1,0:T(8,128)(2,1)S(1)}, u32[]{:S(2)}, u32[]{:S(2)}) collective-permute-start(bf16[2,288,512]{2,1,0:T(8,128)(2,1)S(1)} %pad_maximum_fusion.26), channel_id=1, source_target_pairs={{0,1},{1,0},{2,3},{3,2},{4,5},{5,4},{6,7},{7,6},{8,9},{9,8},{10,11... | collective-permute-start | bytes 1769480 | tf_op jit(solution)/shard_map/ppermute | solution.py:39
  413.3 14.9 %collective-permute-start.61 = (bf16[1,256,512]{2,1,0:T(8,128)(2,1)S(1)}, bf16[1,256,512]{2,1,0:T(8,128)(2,1)S(1)}, u32[]{:S(2)}, u32[]{:S(2)}) collective-permute-start(bf16[1,256,512]{2,1,0:T(8,128)(2,1)S(1)} %fusion.136), channel_id=1, source_target_pairs={{0,2},{1,3},{2,0},{3,1},{4,6},{5,7},{6,4},{7,5},{8,10},{9,11},{10,... | collective-permute-start | bytes 786440 | tf_op jit(solution)/shard_map/ppermute | solution.py:39
  425.0 33.9 %collective-permute-start.39 = (bf16[2,288,512]{2,1,0:T(8,128)(2,1)S(1)}, bf16[2,288,512]{2,1,0:T(8,128)(2,1)S(1)}, u32[]{:S(2)}, u32[]{:S(2)}) collective-permute-start(bf16[2,288,512]{2,1,0:T(8,128)(2,1)S(1)} %pad_maximum_fusion.27), channel_id=1, source_target_pairs={{0,2},{1,3},{2,0},{3,1},{4,6},{5,7},{6,4},{7,5},{8,10},{9,11},{10,... | collective-permute-start | bytes 1769480 | tf_op jit(solution)/shard_map/ppermute | solution.py:39
  428.2 20.3 %collective-permute-start.26 = (bf16[2,288,512]{2,1,0:T(8,128)(2,1)S(1)}, bf16[2,288,512]{2,1,0:T(8,128)(2,1)S(1)}, u32[]{:S(2)}, u32[]{:S(2)}) collective-permute-start(bf16[2,288,512]{2,1,0:T(8,128)(2,1)S(1)} %pad_maximum_fusion.24), channel_id=1, source_target_pairs={{0,1},{1,0},{2,3},{3,2},{4,5},{5,4},{6,7},{7,6},{8,9},{9,8},{10,11... | collective-permute-start | bytes 1769480 | tf_op jit(solution)/shard_map/ppermute | solution.py:39
  429.8 36.4 %collective-permute-start.28 = (bf16[2,288,512]{2,1,0:T(8,128)(2,1)S(1)}, bf16[2,288,512]{2,1,0:T(8,128)(2,1)S(1)}, u32[]{:S(2)}, u32[]{:S(2)}) collective-permute-start(bf16[2,288,512]{2,1,0:T(8,128)(2,1)S(1)} %pad_maximum_fusion.25), channel_id=1, source_target_pairs={{0,2},{1,3},{2,0},{3,1},{4,6},{5,7},{6,4},{7,5},{8,10},{9,11},{10,... | collective-permute-start | bytes 1769480 | tf_op jit(solution)/shard_map/ppermute | solution.py:39
  433.8 20.3 %collective-permute-start.63 = (bf16[1,256,512]{2,1,0:T(8,128)(2,1)S(1)}, bf16[1,256,512]{2,1,0:T(8,128)(2,1)S(1)}, u32[]{:S(2)}, u32[]{:S(2)}) collective-permute-start(bf16[1,256,512]{2,1,0:T(8,128)(2,1)S(1)} %get-tuple-element.182), channel_id=1, source_target_pairs={{0,1},{1,0},{2,3},{3,2},{4,5},{5,4},{6,7},{7,6},{8,9},{9,8},{10,11... | collective-permute-start | bytes 786440 | tf_op jit(solution)/shard_map/ppermute | solution.py:39
  435.9 22.3 %collective-permute-start.52 = (bf16[1,256,512]{2,1,0:T(8,128)(2,1)S(1)}, bf16[1,256,512]{2,1,0:T(8,128)(2,1)S(1)}, u32[]{:S(2)}, u32[]{:S(2)}) collective-permute-start(bf16[1,256,512]{2,1,0:T(8,128)(2,1)S(1)} %get-tuple-element.178), channel_id=1, source_target_pairs={{0,1},{1,0},{2,3},{3,2},{4,5},{5,4},{6,7},{7,6},{8,9},{9,8},{10,11... | collective-permute-start | bytes 786440 | tf_op jit(solution)/shard_map/ppermute | solution.py:39
  448.5 16.9 %collective-permute-start.38 = (bf16[1,288,512]{2,1,0:T(8,128)(2,1)S(1)}, bf16[1,288,512]{2,1,0:T(8,128)(2,1)S(1)}, u32[]{:S(2)}, u32[]{:S(2)}) collective-permute-start(bf16[1,288,512]{2,1,0:T(8,128)(2,1)S(1)} %fusion.124), channel_id=1, source_target_pairs={{0,2},{1,3},{2,0},{3,1},{4,6},{5,7},{6,4},{7,5},{8,10},{9,11},{10,... | collective-permute-start | bytes 884744 | tf_op jit(solution)/shard_map/ppermute | solution.py:39
  454.1 16.3 %collective-permute-start.27 = (bf16[1,288,512]{2,1,0:T(8,128)(2,1)S(1)}, bf16[1,288,512]{2,1,0:T(8,128)(2,1)S(1)}, u32[]{:S(2)}, u32[]{:S(2)}) collective-permute-start(bf16[1,288,512]{2,1,0:T(8,128)(2,1)S(1)} %fusion.130), channel_id=1, source_target_pairs={{0,2},{1,3},{2,0},{3,1},{4,6},{5,7},{6,4},{7,5},{8,10},{9,11},{10,... | collective-permute-start | bytes 884744 | tf_op jit(solution)/shard_map/ppermute | solution.py:39
  471.2 17.3 %collective-permute-start.54 = (bf16[128,512]{1,0:T(8,128)(2,1)S(1)}, bf16[128,512]{1,0:T(8,128)(2,1)S(1)}, u32[]{:S(2)}, u32[]{:S(2)}) collective-permute-start(bf16[128,512]{1,0:T(8,128)(2,1)S(1)} %get-tuple-element.239), channel_id=1, source_target_pairs={{0,8},{4,12},{8,0},{12,4},{1,9},{5,13},{9,1},{13,5},{2,10},{6,14},... | collective-permute-start | bytes 393224 | tf_op jit(solution)/shard_map/ppermute | solution.py:114
  472.6 34.3 %collective-permute-start.40 = (bf16[1,288,512]{2,1,0:T(8,128)(2,1)S(1)}, bf16[1,288,512]{2,1,0:T(8,128)(2,1)S(1)}, u32[]{:S(2)}, u32[]{:S(2)}) collective-permute-start(bf16[1,288,512]{2,1,0:T(8,128)(2,1)S(1)} %get-tuple-element.170), channel_id=1, source_target_pairs={{0,1},{1,0},{2,3},{3,2},{4,5},{5,4},{6,7},{7,6},{8,9},{9,8},{10,11... | collective-permute-start | bytes 884744 | tf_op jit(solution)/shard_map/ppermute | solution.py:39
  476.3 35.3 %collective-permute-start.29 = (bf16[1,288,512]{2,1,0:T(8,128)(2,1)S(1)}, bf16[1,288,512]{2,1,0:T(8,128)(2,1)S(1)}, u32[]{:S(2)}, u32[]{:S(2)}) collective-permute-start(bf16[1,288,512]{2,1,0:T(8,128)(2,1)S(1)} %get-tuple-element.166), channel_id=1, source_target_pairs={{0,1},{1,0},{2,3},{3,2},{4,5},{5,4},{6,7},{7,6},{8,9},{9,8},{10,11... | collective-permute-start | bytes 884744 | tf_op jit(solution)/shard_map/ppermute | solution.py:39
  477.9 22.8 %collective-permute-start.68 = (bf16[128,512]{1,0:T(8,128)(2,1)S(1)}, bf16[128,512]{1,0:T(8,128)(2,1)S(1)}, u32[]{:S(2)}, u32[]{:S(2)}) collective-permute-start(bf16[128,512]{1,0:T(8,128)(2,1)S(1)} %get-tuple-element.137), channel_id=1, source_target_pairs={{0,8},{4,12},{8,0},{12,4},{1,9},{5,13},{9,1},{13,5},{2,10},{6,14},... | collective-permute-start | bytes 393224 | tf_op jit(solution)/shard_map/ppermute | solution.py:120
  488.5 18.0 %collective-permute-start.69 = (bf16[128,512]{1,0:T(8,128)(2,1)S(1)}, bf16[128,512]{1,0:T(8,128)(2,1)S(1)}, u32[]{:S(2)}, u32[]{:S(2)}) collective-permute-start(bf16[128,512]{1,0:T(8,128)(2,1)S(1)} %get-tuple-element.137), channel_id=1, source_target_pairs={{0,12},{4,0},{8,4},{12,8},{1,13},{5,1},{9,5},{13,9},{2,14},{6,2},{... | collective-permute-start | bytes 393224 | tf_op jit(solution)/shard_map/ppermute | solution.py:120
  506.8 55.2 %collective-permute-start.70 = (bf16[512,512]{1,0:T(8,128)(2,1)S(1)}, bf16[512,512]{1,0:T(8,128)(2,1)S(1)}, u32[]{:S(2)}, u32[]{:S(2)}) collective-permute-start(bf16[512,512]{1,0:T(8,128)(2,1)S(1)} %bitcast.579), channel_id=1, source_target_pairs={{0,16},{16,0},{1,17},{17,1},{2,18},{18,2},{3,19},{19,3},{4,20},{20... | collective-permute-start | bytes 1572872 | tf_op jit(solution)/shard_map/ppermute | solution.py:34
  511.1 17.3 %collective-permute-start.42 = (bf16[144,512]{1,0:T(8,128)(2,1)S(1)}, bf16[144,512]{1,0:T(8,128)(2,1)S(1)}, u32[]{:S(2)}, u32[]{:S(2)}) collective-permute-start(bf16[144,512]{1,0:T(8,128)(2,1)S(1)} %get-tuple-element.230), channel_id=1, source_target_pairs={{0,8},{4,12},{8,0},{12,4},{1,9},{5,13},{9,1},{13,5},{2,10},{6,14},... | collective-permute-start | bytes 442376 | tf_op jit(solution)/shard_map/ppermute | solution.py:114
  511.9 16.7 %collective-permute-start.30 = (bf16[144,512]{1,0:T(8,128)(2,1)S(1)}, bf16[144,512]{1,0:T(8,128)(2,1)S(1)}, u32[]{:S(2)}, u32[]{:S(2)}) collective-permute-start(bf16[144,512]{1,0:T(8,128)(2,1)S(1)} %get-tuple-element.223), channel_id=1, source_target_pairs={{0,4},{4,8},{8,12},{12,0},{1,5},{5,9},{9,13},{13,1},{2,6},{6,10},{... | collective-permute-start | bytes 442376 | tf_op jit(solution)/shard_map/ppermute | solution.py:114
  515.9 20.7 %collective-permute-start.32 = (bf16[144,512]{1,0:T(8,128)(2,1)S(1)}, bf16[144,512]{1,0:T(8,128)(2,1)S(1)}, u32[]{:S(2)}, u32[]{:S(2)}) collective-permute-start(bf16[144,512]{1,0:T(8,128)(2,1)S(1)} %get-tuple-element.224), channel_id=1, source_target_pairs={{0,12},{4,0},{8,4},{12,8},{1,13},{5,1},{9,5},{13,9},{2,14},{6,2},{... | collective-permute-start | bytes 442376 | tf_op jit(solution)/shard_map/ppermute | solution.py:114
  521.6 22.5 %collective-permute-start.31 = (bf16[144,512]{1,0:T(8,128)(2,1)S(1)}, bf16[144,512]{1,0:T(8,128)(2,1)S(1)}, u32[]{:S(2)}, u32[]{:S(2)}) collective-permute-start(bf16[144,512]{1,0:T(8,128)(2,1)S(1)} %get-tuple-element.225), channel_id=1, source_target_pairs={{0,8},{4,12},{8,0},{12,4},{1,9},{5,13},{9,1},{13,5},{2,10},{6,14},... | collective-permute-start | bytes 442376 | tf_op jit(solution)/shard_map/ppermute | solution.py:114
  528.6 23.8 %collective-permute-start.45 = (bf16[144,512]{1,0:T(8,128)(2,1)S(1)}, bf16[144,512]{1,0:T(8,128)(2,1)S(1)}, u32[]{:S(2)}, u32[]{:S(2)}) collective-permute-start(bf16[144,512]{1,0:T(8,128)(2,1)S(1)} %get-tuple-element.141), channel_id=1, source_target_pairs={{0,8},{4,12},{8,0},{12,4},{1,9},{5,13},{9,1},{13,5},{2,10},{6,14},... | collective-permute-start | bytes 442376 | tf_op jit(solution)/shard_map/ppermute | solution.py:120
  528.7 15.6 %collective-permute-start.44 = (bf16[144,512]{1,0:T(8,128)(2,1)S(1)}, bf16[144,512]{1,0:T(8,128)(2,1)S(1)}, u32[]{:S(2)}, u32[]{:S(2)}) collective-permute-start(bf16[144,512]{1,0:T(8,128)(2,1)S(1)} %get-tuple-element.141), channel_id=1, source_target_pairs={{0,4},{4,8},{8,12},{12,0},{1,5},{5,9},{9,13},{13,1},{2,6},{6,10},{... | collective-permute-start | bytes 442376 | tf_op jit(solution)/shard_map/ppermute | solution.py:120
  536.6 16.4 %collective-permute-start.46 = (bf16[144,512]{1,0:T(8,128)(2,1)S(1)}, bf16[144,512]{1,0:T(8,128)(2,1)S(1)}, u32[]{:S(2)}, u32[]{:S(2)}) collective-permute-start(bf16[144,512]{1,0:T(8,128)(2,1)S(1)} %get-tuple-element.141), channel_id=1, source_target_pairs={{0,12},{4,0},{8,4},{12,8},{1,13},{5,1},{9,5},{13,9},{2,14},{6,2},{... | collective-permute-start | bytes 442376 | tf_op jit(solution)/shard_map/ppermute | solution.py:120
  544.2 15.7 %collective-permute-start.34 = (bf16[144,512]{1,0:T(8,128)(2,1)S(1)}, bf16[144,512]{1,0:T(8,128)(2,1)S(1)}, u32[]{:S(2)}, u32[]{:S(2)}) collective-permute-start(bf16[144,512]{1,0:T(8,128)(2,1)S(1)} %get-tuple-element.139), channel_id=1, source_target_pairs={{0,8},{4,12},{8,0},{12,4},{1,9},{5,13},{9,1},{13,5},{2,10},{6,14},... | collective-permute-start | bytes 442376 | tf_op jit(solution)/shard_map/ppermute | solution.py:120
  567.6 16.7 %collective-permute-start.75 = (f32[256,512]{1,0:T(8,128)S(1)}, f32[256,512]{1,0:T(8,128)S(1)}, u32[]{:S(2)}, u32[]{:S(2)}) collective-permute-start(f32[256,512]{1,0:T(8,128)S(1)} %get-tuple-element.213), channel_id=1, source_target_pairs={{0,1},{1,0},{2,3},{3,2},{4,5},{5,4},{6,7},{7,6},{8,9},{9,8},{10,11... | collective-permute-start | bytes 1572872 | tf_op jit(solution)/shard_map/ppermute | solution.py:39
  568.9 17.4 %collective-permute-start.77 = (f32[256,512]{1,0:T(8,128)S(1)}, f32[256,512]{1,0:T(8,128)S(1)}, u32[]{:S(2)}, u32[]{:S(2)}) collective-permute-start(f32[256,512]{1,0:T(8,128)S(1)} %get-tuple-element.214), channel_id=1, source_target_pairs={{0,2},{1,3},{2,0},{3,1},{4,6},{5,7},{6,4},{7,5},{8,10},{9,11},{10,... | collective-permute-start | bytes 1572872 | tf_op jit(solution)/shard_map/ppermute | solution.py:39
  573.8 19.8 %collective-permute-start.79 = (f32[256,512]{1,0:T(8,128)S(1)}, f32[256,512]{1,0:T(8,128)S(1)}, u32[]{:S(2)}, u32[]{:S(2)}) collective-permute-start(f32[256,512]{1,0:T(8,128)S(1)} %get-tuple-element.209), channel_id=1, source_target_pairs={{0,1},{1,0},{2,3},{3,2},{4,5},{5,4},{6,7},{7,6},{8,9},{9,8},{10,11... | collective-permute-start | bytes 1572872 | tf_op jit(solution)/shard_map/ppermute | solution.py:39
  574.1 21.6 %collective-permute-start.81 = (f32[256,512]{1,0:T(8,128)S(1)}, f32[256,512]{1,0:T(8,128)S(1)}, u32[]{:S(2)}, u32[]{:S(2)}) collective-permute-start(f32[256,512]{1,0:T(8,128)S(1)} %get-tuple-element.210), channel_id=1, source_target_pairs={{0,2},{1,3},{2,0},{3,1},{4,6},{5,7},{6,4},{7,5},{8,10},{9,11},{10,... | collective-permute-start | bytes 1572872 | tf_op jit(solution)/shard_map/ppermute | solution.py:39
  582.5 22.4 %collective-permute-start.71 = (f32[256,512]{1,0:T(8,128)S(1)}, f32[256,512]{1,0:T(8,128)S(1)}, u32[]{:S(2)}, u32[]{:S(2)}) collective-permute-start(f32[256,512]{1,0:T(8,128)S(1)} %get-tuple-element.217), channel_id=1, source_target_pairs={{0,1},{1,0},{2,3},{3,2},{4,5},{5,4},{6,7},{7,6},{8,9},{9,8},{10,11... | collective-permute-start | bytes 1572872 | tf_op jit(solution)/shard_map/ppermute | solution.py:39
  584.3 22.6 %collective-permute-start.73 = (f32[256,512]{1,0:T(8,128)S(1)}, f32[256,512]{1,0:T(8,128)S(1)}, u32[]{:S(2)}, u32[]{:S(2)}) collective-permute-start(f32[256,512]{1,0:T(8,128)S(1)} %get-tuple-element.218), channel_id=1, source_target_pairs={{0,2},{1,3},{2,0},{3,1},{4,6},{5,7},{6,4},{7,5},{8,10},{9,11},{10,... | collective-permute-start | bytes 1572872 | tf_op jit(solution)/shard_map/ppermute | solution.py:39
  586.6 31.6 %collective-permute-start.76 = (f32[256,512]{1,0:T(8,128)S(1)}, f32[256,512]{1,0:T(8,128)S(1)}, u32[]{:S(2)}, u32[]{:S(2)}) collective-permute-start(f32[256,512]{1,0:T(8,128)S(1)} %get-tuple-element.211), channel_id=1, source_target_pairs={{0,2},{1,3},{2,0},{3,1},{4,6},{5,7},{6,4},{7,5},{8,10},{9,11},{10,... | collective-permute-start | bytes 1572872 | tf_op jit(solution)/shard_map/ppermute | solution.py:39
  593.7 24.9 %collective-permute-start.78 = (f32[256,512]{1,0:T(8,128)S(1)}, f32[256,512]{1,0:T(8,128)S(1)}, u32[]{:S(2)}, u32[]{:S(2)}) collective-permute-start(f32[256,512]{1,0:T(8,128)S(1)} %get-tuple-element.212), channel_id=1, source_target_pairs={{0,1},{1,0},{2,3},{3,2},{4,5},{5,4},{6,7},{7,6},{8,9},{9,8},{10,11... | collective-permute-start | bytes 1572872 | tf_op jit(solution)/shard_map/ppermute | solution.py:39
  596.9 32.6 %collective-permute-start.80 = (f32[256,512]{1,0:T(8,128)}, f32[256,512]{1,0:T(8,128)}, u32[]{:S(2)}, u32[]{:S(2)}) collective-permute-start(f32[256,512]{1,0:T(8,128)} %get-tuple-element.207), channel_id=1, source_target_pairs={{0,2},{1,3},{2,0},{3,1},{4,6},{5,7},{6,4},{7,5},{8,10},{9,11},{10,... | collective-permute-start | bytes 1572872 | tf_op jit(solution)/shard_map/ppermute | solution.py:39
  604.9 31.6 %collective-permute-start.82 = (f32[256,512]{1,0:T(8,128)}, f32[256,512]{1,0:T(8,128)}, u32[]{:S(2)}, u32[]{:S(2)}) collective-permute-start(f32[256,512]{1,0:T(8,128)} %get-tuple-element.208), channel_id=1, source_target_pairs={{0,1},{1,0},{2,3},{3,2},{4,5},{5,4},{6,7},{7,6},{8,9},{9,8},{10,11... | collective-permute-start | bytes 1572872 | tf_op jit(solution)/shard_map/ppermute | solution.py:39
  608.1 94.1 %collective-permute-start.72 = (f32[256,512]{1,0:T(8,128)}, f32[256,512]{1,0:T(8,128)}, u32[]{:S(2)}, u32[]{:S(2)}) collective-permute-start(f32[256,512]{1,0:T(8,128)} %get-tuple-element.215), channel_id=1, source_target_pairs={{0,2},{1,3},{2,0},{3,1},{4,6},{5,7},{6,4},{7,5},{8,10},{9,11},{10,... | collective-permute-start | bytes 1572872 | tf_op jit(solution)/shard_map/ppermute | solution.py:39
  618.2 85.3 %collective-permute-start.74 = (f32[256,512]{1,0:T(8,128)}, f32[256,512]{1,0:T(8,128)}, u32[]{:S(2)}, u32[]{:S(2)}) collective-permute-start(f32[256,512]{1,0:T(8,128)} %get-tuple-element.216), channel_id=1, source_target_pairs={{0,1},{1,0},{2,3},{3,2},{4,5},{5,4},{6,7},{7,6},{8,9},{9,8},{10,11... | collective-permute-start | bytes 1572872 | tf_op jit(solution)/shard_map/ppermute | solution.py:39
  (102 other events, 1656.9 us)
